TPU v7x, 32 devices: a whole 2x2x4 slice. The times are simulated.
32 devices in a mesh: dp: 8 (over z, x), seq: 4 (over y, core).
Axes of the slice: x: 2, y: 2, z: 4, core: 2. Of those that a mesh axis runs over, the one named last changes fastest.
Arguments:
- byte_ids: int32 [16, 2048], P('dp', 'seq'), may hold values from 0 to 258
- lengths: int32 [16], replicated, may hold values from 1 to 2048, 20480 in all
- deal_order: int32 [16], P('dp'), may hold values from 0 to 15, each once
- buckets: int32 [2047], replicated, may hold values from 0 to 31, as said below
- embedding: bfloat16 [259, 768], P(None, 'dp'), may hold values from -6 to 6
- conv_w: bfloat16 [4, 768], P(None, 'dp'), may hold values from -3 to 3
- score_w: bfloat16 [768], P('dp'), may hold values from -0.625 to 0.625
- gain_one: bfloat16 [768], P('dp'), may hold values from 0.5 to 1.5
- w_query: bfloat16 [768, 768], P('dp'), may hold values from -0.109375 to 0.109375
- w_key: bfloat16 [768, 768], P('dp'), may hold values from -0.109375 to 0.109375
- w_value: bfloat16 [768, 768], P('dp'), may hold values from -0.21875 to 0.21875
- w_out: bfloat16 [768, 768], P('dp'), may hold values from -1.25 to 1.25
- rel_bias: bfloat16 [32, 12], replicated, may hold values from -6 to 6
- gain_two: bfloat16 [768], P('dp'), may hold values from 0.5 to 1.5
- w_gate: bfloat16 [768, 2048], P('dp'), may hold values from -0.21875 to 0.21875
- w_up: bfloat16 [768, 2048], P('dp'), may hold values from -0.21875 to 0.21875
- w_down: bfloat16 [2048, 768], P('dp'), may hold values from -0.125 to 0.125
- cotangent: bfloat16 [16, 1024, 768], P('dp', 'seq'), may hold values from -6 to 6
Outputs:
- output: bfloat16 [16, 1024, 768], P('dp', 'seq')
- d_input: bfloat16 [16, 2048, 768], P('dp', 'seq')
- grad_embedding: float32 [259, 768], P(None, 'dp')
- grad_conv: float32 [4, 768], P(None, 'dp')
- grad_score: float32 [768], P('dp')
- grad_gain_one: float32 [768], P('dp')
- grad_query: float32 [768, 768], P('dp')
- grad_key: float32 [768, 768], P('dp')
- grad_value: float32 [768, 768], P('dp')
- grad_out: float32 [768, 768], P('dp')
- grad_rel_bias: float32 [32, 12], replicated
- grad_gain_two: float32 [768], P('dp')
- grad_gate: float32 [768, 2048], P('dp')
- grad_up: float32 [768, 2048], P('dp')
- grad_down: float32 [2048, 768], P('dp')
Inputs may be any that keep to these rules, and one draw needn't show every extreme that they name: Row r holds sequence deal_order[r]; its positions from lengths[deal_order[r]] on are padding; some sequence fills all 2048 positions. `deal_order`: each sequence number appears once. Bidirectional buckets of the offset j - i in the manner of T5: offsets j - i > 0 take the upper 32 / 2 buckets; magnitudes under 32 / 4 each have their own bucket, larger ones fall into ranges spaced by the logarithm up to 128, the edges of each half drawn apart, each edge at T5's or up to a quarter above it, and all magnitudes of 128 or more share the last bucket of their half.
All inputs are finite; a program needn't handle non-finite values.
Results may differ from a plain program's by a relative error of at most 0.019.
Values may be sent and summed in bfloat16 or wider, within the bound.
No kernel may reach another device: no remote copies, remote signals or barrier semaphores. Data moves between devices by JAX's collectives and lax.ppermute only.
A program may use at most 320 MiB of HBM per device.

v0:
```python
import jax
import jax.numpy as jnp
from jax import lax
from jax.sharding import PartitionSpec as P

DH = 64
VOCAB = 259


EPS = 1e-06
NEG = -1000000000.0
HIGH = lax.Precision.HIGHEST


def extended_2(x, sides, width):
    for axis, dim in sides:
        size, length = (lax.axis_size(axis), x.shape[dim])
        up = [(i, (i + 1) % size) for i in range(size - 1)]
        down = [(j, i) for i, j in up]
        last = lax.slice_in_dim(x, length - width, length, axis=dim)
        first = lax.slice_in_dim(x, 0, width, axis=dim)
        before = lax.ppermute(last, axis, up)
        after = lax.ppermute(first, axis, down)
        x = jnp.concatenate([before, x, after], axis=dim)
    return x


def rms_norm(hidden, gain_vec):
    factor = lax.rsqrt(jnp.mean(hidden * hidden, axis=-1, keepdims=True) + EPS)
    return hidden * factor * gain_vec


def geglu(gate_in, upward):
    return jax.nn.gelu(gate_in, approximate=True) * upward


def block_means(padded, offset, extent):
    places = offset + jnp.arange(extent, dtype=jnp.int32)
    results = []
    for block_len in range(1, 5):
        remain = places % block_len
        summed = 0.0
        for shift_at in range(1 - block_len, block_len):
            select = ((shift_at >= -remain) & (shift_at <= block_len - 1 - remain)).astype(
                jnp.float32
            )
            summed = summed + select[:, None] * padded[..., 3 + shift_at : 3 + shift_at + extent, :]
        results.append(summed / block_len)
    return results


def mix_blocks(padded, offset, extent, score_vec):
    averages = block_means(padded, offset, extent)
    scores = jnp.stack([jnp.sum(mean_b * score_vec, axis=-1) for mean_b in averages], axis=0)
    shares = jax.nn.softmax(scores, axis=0)
    pooled = sum((shares[which_b][..., None] * averages[which_b] for which_b in range(4)))
    dims_all = pooled.shape
    return jnp.mean(pooled.reshape(dims_all[:-2] + (dims_all[-2] // 2, 2, dims_all[-1])), axis=-2)


def front_part(extended, conv_vec, score_vec, offset, row_len):
    extent = extended.shape[1] - 8
    conv_out = sum(
        (conv_vec[tap_at] * extended[:, tap_at : tap_at + extent + 4] for tap_at in range(4))
    )
    places = offset - 2 + jnp.arange(extent + 4, dtype=jnp.int32)
    inside = (places[None, :] >= 0) & (places[None, :] < row_len[:, None])
    conv_out = conv_out * inside[:, :, None].astype(jnp.float32)
    padded = jnp.pad(conv_out, ((0, 0), (1, 1), (0, 0)))
    return mix_blocks(padded, offset, extent, score_vec)


def full_skew(bias_rel, keys):
    heads_here = bias_rel.shape[0]
    width = 2 * keys
    window = jnp.pad(bias_rel, ((0, 0), (0, 1)))
    rolled = jnp.roll(window, keys + 1, axis=1)
    tiled = jnp.broadcast_to(rolled[:, None, :], (heads_here, keys, width)).reshape(
        heads_here, keys * width
    )
    return tiled[:, : keys * (width - 1)].reshape(heads_here, keys, width - 1)[:, :, :keys]


def full_unskew(grad_full, keys):
    heads_here = grad_full.shape[0]
    width = 2 * keys
    spread = jnp.pad(grad_full, ((0, 0), (0, 0), (0, width - 1 - keys))).reshape(
        heads_here, keys * (width - 1)
    )
    spread = jnp.pad(spread, ((0, 0), (0, keys))).reshape(heads_here, keys, width)
    folded = jnp.sum(spread, axis=1)
    return jnp.roll(folded, -(keys + 1), axis=1)[:, : width - 1]


def block_scores(query_blk, key_row, bias_full, ok_row, first_row):
    raw = jnp.einsum("qhd,khd->hqk", query_blk, key_row, preferred_element_type=jnp.float32)
    raw = raw + lax.dynamic_slice_in_dim(bias_full, first_row, query_blk.shape[0], 1)
    return jnp.where(ok_row[None, None, :], raw, NEG)


def on_device(
    byte_ids,
    lengths,
    deal_order,
    buckets,
    embedding,
    conv_w,
    score_w,
    gain_one,
    w_query,
    w_key,
    w_value,
    w_out,
    rel_bias,
    gain_two,
    w_gate,
    w_up,
    w_down,
    cotangent,
):
    whole = (
        lax.all_gather(embedding, "dp", axis=1, tiled=True),
        lax.all_gather(conv_w, "dp", axis=1, tiled=True),
        lax.all_gather(score_w, "dp", axis=0, tiled=True),
        lax.all_gather(gain_one, "dp", axis=0, tiled=True),
        lax.all_gather(w_query, "dp", axis=0, tiled=True),
        lax.all_gather(w_key, "dp", axis=0, tiled=True),
        lax.all_gather(w_value, "dp", axis=0, tiled=True),
        lax.all_gather(w_out, "dp", axis=0, tiled=True),
        lax.all_gather(gain_two, "dp", axis=0, tiled=True),
        lax.all_gather(w_gate, "dp", axis=0, tiled=True),
        lax.all_gather(w_up, "dp", axis=0, tiled=True),
        lax.all_gather(w_down, "dp", axis=0, tiled=True),
    )
    (
        emb_all,
        conv_all,
        score_all,
        gain_first,
        query_w,
        key_w,
        value_w,
        out_w,
        gain_second,
        gate_w,
        up_w,
        down_w,
    ) = whole
    rows_dev = byte_ids.shape[0]
    extent = byte_ids.shape[1]
    offset = lax.axis_index("seq") * extent
    matches = deal_order[:, None] == jnp.arange(lengths.shape[0], dtype=jnp.int32)[None, :]
    row_len = jnp.sum(jnp.where(matches, lengths[None, :], 0), axis=1)
    places = offset + jnp.arange(extent, dtype=jnp.int32)
    live = (places[None, :] < row_len[:, None]).astype(jnp.bfloat16)[:, :, None]
    embedded = jnp.take(emb_all, byte_ids, axis=0)
    masked = embedded * live
    extended = extended_2(masked, (("seq", 1),), 4)

    def front_call(ext_in, conv_in, score_in):
        return front_part(ext_in, conv_in, score_in, offset, row_len)

    h_zero, front_back = jax.vjp(
        front_call,
        extended.astype(jnp.float32),
        conv_all.astype(jnp.float32),
        score_all.astype(jnp.float32),
    )
    normed_one, norm_one_back = jax.vjp(rms_norm, h_zero, gain_first.astype(jnp.float32))
    low_one = normed_one.astype(jnp.bfloat16)
    query_tok = jnp.dot(low_one, query_w, preferred_element_type=jnp.float32).astype(jnp.bfloat16)
    key_tok = jnp.dot(low_one, key_w, preferred_element_type=jnp.float32).astype(jnp.bfloat16)
    value_tok = jnp.dot(low_one, value_w, preferred_element_type=jnp.float32).astype(jnp.bfloat16)
    query_heads, key_heads, value_heads = (
        lax.all_to_all(query_tok, "seq", split_axis=2, concat_axis=1, tiled=True),
        lax.all_to_all(key_tok, "seq", split_axis=2, concat_axis=1, tiled=True),
        lax.all_to_all(value_tok, "seq", split_axis=2, concat_axis=1, tiled=True),
    )
    seq_len = query_heads.shape[1]
    heads_dev = query_heads.shape[2] // DH
    blk_rows = min(512, seq_len)
    starts = jnp.arange(seq_len // blk_rows, dtype=jnp.int32) * blk_rows
    first_head = lax.axis_index("seq") * heads_dev
    bias_loc = lax.dynamic_slice_in_dim(rel_bias.astype(jnp.float32), first_head, heads_dev, 1)
    onehot = (buckets[:, None] == jnp.arange(rel_bias.shape[0], dtype=jnp.int32)[None, :]).astype(
        jnp.float32
    )
    bias_rel = jnp.dot(onehot, bias_loc, precision=HIGH).T
    bias_full = full_skew(bias_rel, seq_len)
    key_ok = 2 * jnp.arange(seq_len, dtype=jnp.int32)[None, :] < row_len[:, None]
    query_4 = query_heads.reshape(rows_dev, seq_len, heads_dev, DH)
    key_4 = key_heads.reshape(rows_dev, seq_len, heads_dev, DH)
    value_4 = value_heads.reshape(rows_dev, seq_len, heads_dev, DH)

    def attend_row(row_args):
        query_row, key_row, value_row, ok_row = row_args

        def attend_one_block(first_row):
            query_blk = lax.dynamic_slice_in_dim(query_row, first_row, blk_rows, 0)
            scores = block_scores(query_blk, key_row, bias_full, ok_row, first_row)
            top_val = jnp.max(scores, axis=-1, keepdims=True)
            weights_raw = jnp.exp(scores - top_val)
            totals = jnp.sum(weights_raw, axis=-1, keepdims=True)
            prob_low = (weights_raw / totals).astype(jnp.bfloat16)
            log_part = (top_val + jnp.log(totals))[..., 0]
            result = jnp.einsum(
                "hqk,khd->qhd", prob_low, value_row, preferred_element_type=jnp.float32
            )
            return (result.astype(jnp.bfloat16), log_part)

        blocks_out, log_parts = lax.map(attend_one_block, starts)
        return (blocks_out.reshape(seq_len, heads_dev * DH), log_parts)

    attended_heads, log_sums = lax.map(attend_row, (query_4, key_4, value_4, key_ok))
    attended = lax.all_to_all(attended_heads, "seq", split_axis=1, concat_axis=2, tiled=True)
    h_one = h_zero + jnp.dot(attended, out_w, preferred_element_type=jnp.float32)
    normed_two, norm_two_back = jax.vjp(rms_norm, h_one, gain_second.astype(jnp.float32))
    low_two = normed_two.astype(jnp.bfloat16)
    gate_val = jnp.dot(low_two, gate_w, preferred_element_type=jnp.float32)
    up_val = jnp.dot(low_two, up_w, preferred_element_type=jnp.float32)
    mixed_ff, ff_back = jax.vjp(geglu, gate_val, up_val)
    hidden = mixed_ff.astype(jnp.bfloat16)
    output = (h_one + jnp.dot(hidden, down_w, preferred_element_type=jnp.float32)).astype(
        jnp.bfloat16
    )
    query_b, key_b, value_b, out_b = (query_w, key_w, value_w, out_w)
    gate_b, up_b, down_b = (gate_w, up_w, down_w)
    grad_down = jnp.einsum("gtf,gtd->fd", hidden, cotangent, preferred_element_type=jnp.float32)
    d_hidden = jnp.einsum("gtd,fd->gtf", cotangent, down_b, preferred_element_type=jnp.float32)
    d_gate_f, d_up_f = ff_back(d_hidden)
    d_gate = d_gate_f.astype(jnp.bfloat16)
    d_up = d_up_f.astype(jnp.bfloat16)
    grad_gate = jnp.einsum("gtd,gtf->df", low_two, d_gate, preferred_element_type=jnp.float32)
    grad_up = jnp.einsum("gtd,gtf->df", low_two, d_up, preferred_element_type=jnp.float32)
    d_norm_two = jnp.einsum("gtf,df->gtd", d_gate, gate_b, preferred_element_type=jnp.float32)
    d_norm_two = d_norm_two + jnp.einsum(
        "gtf,df->gtd", d_up, up_b, preferred_element_type=jnp.float32
    )
    d_h_norm, grad_gain_two = norm_two_back(d_norm_two)
    d_h_one = cotangent.astype(jnp.float32) + d_h_norm
    d_branch = d_h_one.astype(jnp.bfloat16)
    grad_out = jnp.einsum("gtd,gte->de", attended, d_branch, preferred_element_type=jnp.float32)
    d_attended = jnp.einsum(
        "gte,de->gtd", d_branch, out_b, preferred_element_type=jnp.float32
    ).astype(jnp.bfloat16)
    d_heads = lax.all_to_all(d_attended, "seq", split_axis=2, concat_axis=1, tiled=True)
    d_heads_4 = d_heads.reshape(rows_dev, seq_len, heads_dev, DH)

    def row_grads(row_args):
        query_row, key_row, value_row, ok_row, log_row, dout_row = row_args

        def row_one_block(running, scan_item):
            d_keys, d_values, d_full = running
            first_row, log_blk = scan_item
            query_blk = lax.dynamic_slice_in_dim(query_row, first_row, blk_rows, 0)
            dout_blk = lax.dynamic_slice_in_dim(dout_row, first_row, blk_rows, 0)
            scores = block_scores(query_blk, key_row, bias_full, ok_row, first_row)
            prob_f = jnp.exp(scores - log_blk[:, :, None])
            prob_low = prob_f.astype(jnp.bfloat16)
            d_probs = jnp.einsum(
                "qhd,khd->hqk", dout_blk, value_row, preferred_element_type=jnp.float32
            )
            inner = jnp.sum(prob_f * d_probs, axis=-1, keepdims=True)
            d_scores = (prob_f * (d_probs - inner)).astype(jnp.bfloat16)
            d_query = jnp.einsum(
                "hqk,khd->qhd", d_scores, key_row, preferred_element_type=jnp.float32
            )
            d_keys = d_keys + jnp.einsum(
                "hqk,qhd->khd", d_scores, query_blk, preferred_element_type=jnp.float32
            )
            d_values = d_values + jnp.einsum(
                "hqk,qhd->khd", prob_low, dout_blk, preferred_element_type=jnp.float32
            )
            d_full = lax.dynamic_update_slice_in_dim(
                d_full, d_scores.astype(jnp.float32), first_row, 1
            )
            return ((d_keys, d_values, d_full), d_query.astype(jnp.bfloat16))

        start_sums = (
            jnp.zeros((seq_len, heads_dev, DH), jnp.float32),
            jnp.zeros((seq_len, heads_dev, DH), jnp.float32),
            jnp.zeros((heads_dev, seq_len, seq_len), jnp.float32),
        )
        (d_keys, d_values, d_full), d_queries = lax.scan(
            row_one_block, start_sums, (starts, log_row)
        )
        return (
            d_queries.reshape(seq_len, heads_dev * DH),
            d_keys.astype(jnp.bfloat16).reshape(seq_len, heads_dev * DH),
            d_values.astype(jnp.bfloat16).reshape(seq_len, heads_dev * DH),
            d_full,
        )

    d_query_h, d_key_h, d_value_h, d_full_rows = lax.map(
        row_grads, (query_4, key_4, value_4, key_ok, log_sums, d_heads_4)
    )
    d_query_t, d_key_t, d_value_t = (
        lax.all_to_all(d_query_h, "seq", split_axis=1, concat_axis=2, tiled=True),
        lax.all_to_all(d_key_h, "seq", split_axis=1, concat_axis=2, tiled=True),
        lax.all_to_all(d_value_h, "seq", split_axis=1, concat_axis=2, tiled=True),
    )
    grad_query = jnp.einsum("gtd,gte->de", low_one, d_query_t, preferred_element_type=jnp.float32)
    grad_key = jnp.einsum("gtd,gte->de", low_one, d_key_t, preferred_element_type=jnp.float32)
    grad_value = jnp.einsum("gtd,gte->de", low_one, d_value_t, preferred_element_type=jnp.float32)
    d_norm_one = jnp.einsum("gte,de->gtd", d_query_t, query_b, preferred_element_type=jnp.float32)
    d_norm_one = d_norm_one + jnp.einsum(
        "gte,de->gtd", d_key_t, key_b, preferred_element_type=jnp.float32
    )
    d_norm_one = d_norm_one + jnp.einsum(
        "gte,de->gtd", d_value_t, value_b, preferred_element_type=jnp.float32
    )
    d_h_first, grad_gain_one = norm_one_back(d_norm_one)
    d_h_zero = d_h_one + d_h_first
    d_ext, grad_conv, grad_score = front_back(d_h_zero)
    rim_out = jnp.concatenate([d_ext[:, :4], d_ext[:, -4:]], axis=1)
    rim_in = extended_2(rim_out.astype(jnp.bfloat16), (("seq", 1),), 4).astype(rim_out.dtype)
    d_masked = d_ext[:, 4:-4] + jnp.pad(rim_in[:, :4], ((0, 0), (0, extent - 4), (0, 0)))
    d_masked = d_masked + jnp.pad(rim_in[:, 12:], ((0, 0), (extent - 4, 0), (0, 0)))
    d_input = (d_masked * live.astype(jnp.float32)).astype(jnp.bfloat16)
    grad_embedding = jax.ops.segment_sum(
        d_input.astype(jnp.float32).reshape(-1, d_input.shape[2]),
        byte_ids.reshape(-1),
        num_segments=VOCAB,
    )
    d_bias_all = full_unskew(jnp.sum(d_full_rows, axis=0), seq_len)
    d_rel_loc = jnp.dot(onehot.T, d_bias_all.T, precision=HIGH)
    d_rel_full = lax.dynamic_update_slice_in_dim(
        jnp.zeros(rel_bias.shape, jnp.float32), d_rel_loc, first_head, 1
    )
    grad_rel_bias = lax.psum(d_rel_full, ("dp", "seq"))
    partial_sums = (
        lax.psum_scatter(grad_embedding, "dp", scatter_dimension=1, tiled=True),
        lax.psum_scatter(grad_conv, "dp", scatter_dimension=1, tiled=True),
        lax.psum_scatter(grad_score, "dp", scatter_dimension=0, tiled=True),
        lax.psum_scatter(grad_gain_one, "dp", scatter_dimension=0, tiled=True),
        lax.psum_scatter(grad_query, "dp", scatter_dimension=0, tiled=True),
        lax.psum_scatter(grad_key, "dp", scatter_dimension=0, tiled=True),
        lax.psum_scatter(grad_value, "dp", scatter_dimension=0, tiled=True),
        lax.psum_scatter(grad_out, "dp", scatter_dimension=0, tiled=True),
        lax.psum_scatter(grad_gain_two, "dp", scatter_dimension=0, tiled=True),
        lax.psum_scatter(grad_gate, "dp", scatter_dimension=0, tiled=True),
        lax.psum_scatter(grad_up, "dp", scatter_dimension=0, tiled=True),
        lax.psum_scatter(grad_down, "dp", scatter_dimension=0, tiled=True),
    )
    owned = (
        lax.psum(partial_sums[0].astype(jnp.bfloat16), "seq").astype(jnp.float32),
        lax.psum(partial_sums[1].astype(jnp.bfloat16), "seq").astype(jnp.float32),
        lax.psum(partial_sums[2].astype(jnp.bfloat16), "seq").astype(jnp.float32),
        lax.psum(partial_sums[3].astype(jnp.bfloat16), "seq").astype(jnp.float32),
        lax.psum(partial_sums[4].astype(jnp.bfloat16), "seq").astype(jnp.float32),
        lax.psum(partial_sums[5].astype(jnp.bfloat16), "seq").astype(jnp.float32),
        lax.psum(partial_sums[6].astype(jnp.bfloat16), "seq").astype(jnp.float32),
        lax.psum(partial_sums[7].astype(jnp.bfloat16), "seq").astype(jnp.float32),
        lax.psum(partial_sums[8].astype(jnp.bfloat16), "seq").astype(jnp.float32),
        lax.psum(partial_sums[9].astype(jnp.bfloat16), "seq").astype(jnp.float32),
        lax.psum(partial_sums[10].astype(jnp.bfloat16), "seq").astype(jnp.float32),
        lax.psum(partial_sums[11].astype(jnp.bfloat16), "seq").astype(jnp.float32),
    )
    g_emb, g_conv, g_score, g_one, g_query, g_key, g_value, g_out, g_two, g_gate, g_up, g_down = (
        owned
    )
    return (
        output,
        d_input,
        g_emb,
        g_conv,
        g_score,
        g_one,
        g_query,
        g_key,
        g_value,
        g_out,
        grad_rel_bias,
        g_two,
        g_gate,
        g_up,
        g_down,
    )


def solution(mesh):
    return jax.shard_map(
        on_device,
        mesh=mesh,
        in_specs=(
            P("dp", "seq"),
            P(),
            P("dp"),
            P(),
            P(None, "dp"),
            P(None, "dp"),
            P("dp"),
            P("dp"),
            P("dp", None),
            P("dp", None),
            P("dp", None),
            P("dp", None),
            P(),
            P("dp"),
            P("dp", None),
            P("dp", None),
            P("dp", None),
            P("dp", "seq", None),
        ),
        out_specs=(
            P("dp", "seq", None),
            P("dp", "seq", None),
            P(None, "dp"),
            P(None, "dp"),
            P("dp"),
            P("dp"),
            P("dp", None),
            P("dp", None),
            P("dp", None),
            P("dp", None),
            P(),
            P("dp"),
            P("dp", None),
            P("dp", None),
            P("dp", None),
        ),
        check_vma=False,
    )
```

profile of v0, /device:TPU:0, one launch (start us, length us, event | category | flops | bytes accessed | tf_op | source)
XLA Modules:
  0.0 2029.9 jit_solution(16420635852990077017)
XLA Ops:
  11.2 33.7 %all-gather.1 = bf16[8,96,259]{1,2,0:T(8,128)(2,1)S(1)} all-gather(bf16[1,96,259]{1,2,0:T(8,128)(2,1)} %bitcast.333), channel_id=1, replica_groups=mesh['dp'=8,'seq'=4] {'dp'}, dimensions={0}, use_global_device_ids=true | all-gather | bytes 447552 | tf_op jit(solution)/shard_map/all_gather | solution.py:122
  141.9 33.4 %copy.248 = f32[1,3,1024,2048]{3,1,2,0:T(4,128)} copy(f32[1,3,1024,2048]{3,2,1,0:T(8,128)} %broadcast_bitcast_fusion) | data formatting | bytes 50331648
  182.7 23.2 %slice_bitcast_fusion.8 = f32[1,3,2096128]{2,1,0:T(4,128)} fusion(f32[3,2097152]{1,0:T(4,128)} %bitcast.302), kind=kLoop, calls=%fused_computation.322 | loop fusion | bytes 50307072
  214.0 466.9 %while.67 = (u32[]{:T(128)}, f32[1,3,2096128]{2,1,0:T(4,128)}, f32[6288384]{0:T(1024)}, u32[]{}, f32[]{:T(128)}, /*index=5*/u32[]{}, u32[]{}, u32[]{}) while((u32[]{:T(128)}, f32[1,3,2096128]{2,1,0:T(4,128)}, f32[6288384]{0:T(1024)}, u32[]{}, f32[]{:T(128)}, /*index=5*/u32[]{}, u32[]{}, u32[]{}) %tuple.205), condition=%wide.cond, body=%wide.body.sunk | while | flops 9 | bytes 33538248
  214.6 83.8 %dynamic-slice_reduce_fusion.8 = f32[2096128]{0:T(1024)} fusion(f32[]{:T(128)} %broadcast.1119, f32[1,3,2096128]{2,1,0:T(4,128)} %get-tuple-element.1108, u32[]{:T(128)S(6)} %multiply.119, u32[]{:T(128)S(6)} %multiply.120), kind=kLoop, calls=%fused_computation.321.clone.1 | loop fusion | bytes 16769036
  298.4 71.4 %dynamic-update-slice.7 = f32[6288384]{0:T(1024)} dynamic-update-slice(f32[6288384]{0:T(1024)} %get-tuple-element.1101, f32[2096128]{0:T(1024)} %dynamic-slice_reduce_fusion.8, u32[]{:T(128)S(6)} %add.984) | dynamic-update-slice | bytes 16769028
  370.3 83.8 %dynamic-slice_reduce_fusion.8 = f32[2096128]{0:T(1024)} fusion(f32[]{:T(128)} %broadcast.1119, f32[1,3,2096128]{2,1,0:T(4,128)} %get-tuple-element.1108, u32[]{:T(128)S(6)} %multiply.119, u32[]{:T(128)S(6)} %multiply.120), kind=kLoop, calls=%fused_computation.321.clone.1 | loop fusion | bytes 16769036
  454.1 71.3 %dynamic-update-slice.7 = f32[6288384]{0:T(1024)} dynamic-update-slice(f32[6288384]{0:T(1024)} %get-tuple-element.1101, f32[2096128]{0:T(1024)} %dynamic-slice_reduce_fusion.8, u32[]{:T(128)S(6)} %add.984) | dynamic-update-slice | bytes 16769028
  525.9 83.8 %dynamic-slice_reduce_fusion.8 = f32[2096128]{0:T(1024)} fusion(f32[]{:T(128)} %broadcast.1119, f32[1,3,2096128]{2,1,0:T(4,128)} %get-tuple-element.1108, u32[]{:T(128)S(6)} %multiply.119, u32[]{:T(128)S(6)} %multiply.120), kind=kLoop, calls=%fused_computation.321.clone.1 | loop fusion | bytes 16769036
  609.7 71.2 %dynamic-update-slice.7 = f32[6288384]{0:T(1024)} dynamic-update-slice(f32[6288384]{0:T(1024)} %get-tuple-element.1101, f32[2096128]{0:T(1024)} %dynamic-slice_reduce_fusion.8, u32[]{:T(128)S(6)} %add.984) | dynamic-update-slice | bytes 16769028
  681.0 37.5 %reshape.487 = f32[3,1024,2047]{2,1,0:T(8,128)} reshape(f32[6288384]{0:T(1024)} %get-tuple-element.378) | data formatting | bytes 50307072 | tf_op jit(solution)/shard_map/reshape | solution.py:81
  736.5 49.9 %while.64 = (s32[]{:T(128)}, bf16[2,1024,192]{1,2,0:T(8,128)(2,1)}, f32[2,2,3,512]{3,2,1,0:T(4,128)}, bf16[2,1024,3,64]{1,3,2,0:T(8,128)(2,1)S(1)}, bf16[2,1024,...) while((s32[]{:T(128)}, bf16[2,1024,192]{1,2,0:T(8,128)(2,1)}, ...), condition=%wide.region_13.14_spmd.clone, body=%wide.region_8.13_spmd.clone.sunk | while | flops 415332864 | bytes 32832016 | solution.py:214
  875.1 241.7 %while.66 = (s32[]{:T(128)}, bf16[2,1024,192]{1,2,0:T(8,128)(2,1)}, bf16[2,1024,192]{1,2,0:T(8,128)(2,1)}, bf16[2,1024,192]{1,2,0:T(8,128)(2,1)}, f32[2,3,1024,1...) while((s32[]{:T(128)}, bf16[2,1024,192]{1,2,0:T(8,128)(2,1)}, ...), condition=%wide.region_20.21_spmd.clone, body=%wide.region_16.20_spmd.clone.sunk | while | flops 1023638016 | bytes 235006976 | solution.py:294
  885.7 93.4 %while.70 = (s32[]{:T(128)}, f32[1024,3,64]{0,2,1:T(8,128)}, f32[1024,3,64]{0,2,1:T(8,128)}, f32[3,1024,1024]{2,1,0:T(8,128)}, bf16[2,512,3,64]{1,3,2,0:T(8,128)...) while((s32[]{:T(128)}, f32[1024,3,64]{0,2,1:T(8,128)}, ...), condition=%wide.region_19.19_spmd.clone, body=%wide.region_17.18_spmd.clone.sunk | while | flops 1023244800 | bytes 153190736 | solution.py:284
  1006.8 93.1 %while.70 = (s32[]{:T(128)}, f32[1024,3,64]{0,2,1:T(8,128)}, f32[1024,3,64]{0,2,1:T(8,128)}, f32[3,1024,1024]{2,1,0:T(8,128)}, bf16[2,512,3,64]{1,3,2,0:T(8,128)...) while((s32[]{:T(128)}, f32[1024,3,64]{0,2,1:T(8,128)}, ...), condition=%wide.region_19.19_spmd.clone, body=%wide.region_17.18_spmd.clone.sunk | while | flops 1023244800 | bytes 153190736 | solution.py:284
  1326.1 34.8 %reshape.566 = f32[6288384]{0:T(1024)} reshape(f32[3,1024,2047]{2,1,0:T(8,128)} %pad.146) | data formatting | bytes 50307072
  1360.9 492.9 %while.68 = (u32[]{:T(128)}, f32[6288384]{0:T(1024)}, f32[1,3,2096128]{2,1,0:T(4,128)}, u32[]{}, u32[]{}, /*index=5*/u32[]{}, u32[]{}, u32[]{}) while((u32[]{:T(128)}, f32[6288384]{0:T(1024)}, f32[1,3,2096128]{2,1,0:T(4,128)}, u32[]{}, u32[]{}, /*index=5*/u32[]{}, u32[]{}, u32[]{}) %tuple.214), condition=%wide.cond.1, body=%wide.body.1.sunk | while | flops 9 | bytes 50307256
  1373.8 151.3 %dynamic-update-slice.8 = f32[1,3,2096128]{2,1,0:T(4,128)} dynamic-update-slice(f32[1,3,2096128]{2,1,0:T(4,128)} %get-tuple-element.1218, f32[1,1,2096128]{2,1,0:T(1,128)} %reshape.569, u32[]{:T(128)S(6)} %multiply.123, u32[]{:T(128)S(6)} %multiply.125, u32[]{} %constant.558..sunk) | dynamic-update-slice | bytes 16769028
  1537.9 151.7 %dynamic-update-slice.8 = f32[1,3,2096128]{2,1,0:T(4,128)} dynamic-update-slice(f32[1,3,2096128]{2,1,0:T(4,128)} %get-tuple-element.1218, f32[1,1,2096128]{2,1,0:T(1,128)} %reshape.569, u32[]{:T(128)S(6)} %multiply.123, u32[]{:T(128)S(6)} %multiply.125, u32[]{} %constant.558..sunk) | dynamic-update-slice | bytes 16769028
  1702.5 151.3 %dynamic-update-slice.8 = f32[1,3,2096128]{2,1,0:T(4,128)} dynamic-update-slice(f32[1,3,2096128]{2,1,0:T(4,128)} %get-tuple-element.1218, f32[1,1,2096128]{2,1,0:T(1,128)} %reshape.569, u32[]{:T(128)S(6)} %multiply.123, u32[]{:T(128)S(6)} %multiply.125, u32[]{} %constant.558..sunk) | dynamic-update-slice | bytes 16769028
  1853.8 22.7 %pad.147 = f32[3,2097152]{1,0:T(4,128)} pad(f32[3,2096128]{1,0:T(4,128)} %bitcast.305, f32[]{:T(128)} %constant.209.clone.1), padding=0_0x0_1024 | pad | bytes 50319364 | tf_op jit(solution)/shard_map/jit(_pad)/pad | solution.py:90
  1876.5 26.3 %bitcast_reduce_fusion = f32[3,2048]{1,0:T(4,128)S(1)} fusion(f32[1,3,1024,2048]{3,1,2,0:T(4,128)} %bitcast.301), kind=kLoop, calls=%fused_computation.55 | loop fusion | flops 6285312 | bytes 25190400 | tf_op jit(solution)/shard_map/reduce_sum | solution.py:91
  1903.6 39.6 %psum.99 = f32[32,12]{0,1:T(8,128)} all-reduce(f32[32,12]{0,1:T(8,128)S(1)} %dynamic_update_slice.38), channel_id=1, replica_groups=mesh['dp'=8,'seq'=4] {'dp','seq'}, use_global_device_ids=true, to_apply=%region_55.56 | all-reduce | flops 384 | bytes 3072 | tf_op jit(solution)/shard_map/psum | solution.py:330
  1959.0 36.9 %all-reduce.40 = (bf16[768]{0:T(1024)(128)(2,1)S(1)}, bf16[768]{0:T(1024)(128)(2,1)S(1)}, bf16[768]{0:T(1024)(128)(2,1)S(1)}) all-reduce(f32[768]{0:T(1024)S(1)} %add_add_fusion.3, f32[768]{0:T(1024)S(1)} %copy-done.85, f32[768]{0:T(1024)S(1)} %copy-done.92), channel_id=4, replica_groups=mesh['dp'=8,'seq'=4] {'dp'}, use_global_device_ids=true, to_apply=%region_40.41.clone | all-reduce | flops 2304 | bytes 13824
  (657 shorter events, 830.5 us)
Async XLA Ops:
  7.2 115.3 %all-gather.10.cloned.1.call-start = ((), (), s32[]{:S(2)}) async-start(), calls=%async_computation.17 | async-start | bytes 1327104 | tf_op jit(solution)/shard_map/all_gather | solution.py:126
  7.9 167.4 %all-gather.12.cloned.1.call-start = ((), (), s32[]{:S(2)}) async-start(), calls=%async_computation.18 | async-start | bytes 1327104 | tf_op jit(solution)/shard_map/all_gather | solution.py:127
  8.7 197.2 %all-gather.14.cloned.1.call-start = ((), (), s32[]{:S(2)}) async-start(), calls=%async_computation.19 | async-start | bytes 1327104 | tf_op jit(solution)/shard_map/all_gather | solution.py:128
  9.4 806.5 %all-gather.16.cloned.1.call-start = ((), (), s32[]{:S(2)}) async-start(), calls=%async_computation.20 | async-start | bytes 1327104 | tf_op jit(solution)/shard_map/all_gather | solution.py:129
  10.0 809.8 %all-gather.22.cloned.1.call-start = ((), (), s32[]{:S(2)}) async-start(), calls=%async_computation.23 | async-start | bytes 3538944 | tf_op jit(solution)/shard_map/all_gather | solution.py:133
  10.6 815.4 %all-gather.20.cloned.1.call-start = ((), (), s32[]{:S(2)}) async-start(), calls=%async_computation.22 | async-start | bytes 3538944 | tf_op jit(solution)/shard_map/all_gather | solution.py:132
  11.2 820.6 %all-gather.18.cloned.1.call-start = ((), (), s32[]{:S(2)}) async-start(), calls=%async_computation.21 | async-start | bytes 3538944 | tf_op jit(solution)/shard_map/all_gather | solution.py:131
  50.9 46.5 %collective-permute-start.1 = (bf16[2,4,768]{2,1,0:T(4,128)(2,1)S(1)}, bf16[2,4,768]{2,1,0:T(4,128)(2,1)S(1)}, u32[]{:S(2)}, u32[]{:S(2)}) collective-permute-start(bf16[2,4,768]{2,1,0:T(4,128)(2,1)S(1)} %get-tuple-element.573), channel_id=1, source_target_pairs={{1,0},{2,1},{3,2},{5,4},{6,5},{7,6},{9,8},{10,9},{11,10},{13,12},{... | collective-permute-start | bytes 36872 | tf_op jit(solution)/shard_map/ppermute | solution.py:23
  52.2 45.2 %collective-permute-start = (bf16[2,4,768]{2,1,0:T(4,128)(2,1)S(1)}, bf16[2,4,768]{2,1,0:T(4,128)(2,1)S(1)}, u32[]{:S(2)}, u32[]{:S(2)}) collective-permute-start(bf16[2,4,768]{2,1,0:T(4,128)(2,1)S(1)} %get-tuple-element.572), channel_id=1, source_target_pairs={{0,1},{1,2},{2,3},{4,5},{5,6},{6,7},{8,9},{9,10},{10,11},{12,13},{... | collective-permute-start | bytes 36872 | tf_op jit(solution)/shard_map/ppermute | solution.py:22
  126.7 52.5 %all-to-all-start = ((bf16[2,256,768]{1,0,2:T(2,128)(2,1)}), bf16[2,256,768]{1,0,2:T(2,128)(2,1)S(1)}, u32[]{:S(2)}, u32[]{:S(2)}) async-start(bf16[2,256,768]{1,0,2:T(2,128)(2,1)} %copy.189), calls=%async_computation | async-start | bytes 1572864 | tf_op jit(solution)/shard_map/all_to_all | solution.py:175
  179.2 30.6 %all-to-all-start.1 = ((bf16[2,256,768]{1,0,2:T(2,128)(2,1)}), bf16[2,256,768]{1,0,2:T(2,128)(2,1)S(1)}, u32[]{:S(2)}, u32[]{:S(2)}) async-start(bf16[2,256,768]{1,0,2:T(2,128)(2,1)} %copy.192), calls=%async_computation.1 | async-start | bytes 1572864 | tf_op jit(solution)/shard_map/all_to_all | solution.py:176
  209.8 523.4 %all-to-all-start.2 = ((bf16[2,256,768]{1,0,2:T(2,128)(2,1)}), bf16[2,256,768]{1,0,2:T(2,128)(2,1)}, u32[]{:S(2)}, u32[]{:S(2)}) async-start(bf16[2,256,768]{1,0,2:T(2,128)(2,1)} %copy.195), calls=%async_computation.2 | async-start | bytes 1572864 | tf_op jit(solution)/shard_map/all_to_all | solution.py:177
  790.9 19.1 all-to-all-start.3
  853.9 15.9 all-to-all-start.4
  858.1 1085.2 %reduce-scatter.20.cloned.1.call-start = ((), (), s32[]{:S(2)}) async-start(), calls=%async_computation.27 | async-start | bytes 2654208 | tf_op jit(solution)/shard_map/reduce_scatter | solution.py:339
  861.5 1083.4 %reduce-scatter.14.cloned.1.call-start = ((), (), s32[]{:S(2)}) async-start(), calls=%async_computation.24 | async-start | bytes 2654208 | tf_op jit(solution)/shard_map/reduce_scatter | solution.py:336
  1141.7 804.8 %reduce-scatter.16.cloned.1.call-start = ((), (), s32[]{:S(2)}) async-start(), calls=%async_computation.25 | async-start | bytes 2654208 | tf_op jit(solution)/shard_map/reduce_scatter | solution.py:337
  1164.8 783.5 %reduce-scatter.18.cloned.1.call-start = ((), (), s32[]{:S(2)}) async-start(), calls=%async_computation.26 | async-start | bytes 2654208 | tf_op jit(solution)/shard_map/reduce_scatter | solution.py:338
  1186.9 762.9 %reduce-scatter.22.cloned.1.call-start = ((), (), s32[]{:S(2)}) async-start(), calls=%async_computation.28 | async-start | bytes 7077888 | tf_op jit(solution)/shard_map/reduce_scatter | solution.py:341
  1193.2 758.6 %reduce-scatter.24.cloned.1.call-start = ((), (), s32[]{:S(2)}) async-start(), calls=%async_computation.29 | async-start | bytes 7077888 | tf_op jit(solution)/shard_map/reduce_scatter | solution.py:342
  1199.3 754.4 %reduce-scatter.26.cloned.1.call-start = ((), (), s32[]{:S(2)}) async-start(), calls=%async_computation.30 | async-start | bytes 7077888 | tf_op jit(solution)/shard_map/reduce_scatter | solution.py:343
  1206.6 789.5 %reduce-scatter.30.cloned.1.call-start = ((), (), s32[]{:S(2)}) async-start(), calls=%async_computation.32 | async-start | bytes 442368
  1277.0 719.9 %reduce-scatter.28.cloned.1.call-start = ((), (), s32[]{:S(2)}) async-start(), calls=%async_computation.31 | async-start | bytes 1327104
  1290.5 722.2 %all-reduce.46.cloned.1.call-start = ((), (), s32[]{:S(2)}) async-start(), calls=%async_computation.33 | async-start | bytes 3538944 | tf_op jit(solution)/shard_map/psum | solution.py:350
  (136 other events, 1060.7 us)
Sparse Core Ops, SparseCore 0:
  10.2 45.1 all-gather.9
  57.6 40.3 all-gather.11
  100.2 39.8 all-gather.13
  142.1 39.8 all-gather.15
  184.0 59.2 all-gather.21
  245.3 59.0 all-gather.19
  306.6 59.0 all-gather.17
  862.4 68.1 reduce-scatter.19
  1141.9 66.5 reduce-scatter.13
  1211.8 68.0 reduce-scatter.15
  1283.4 68.0 reduce-scatter.17
  1354.9 116.9 reduce-scatter.21
  1475.6 117.0 reduce-scatter.23
  1596.1 117.0 reduce-scatter.25
  1716.9 60.5 reduce-scatter.29
  1780.7 63.2 reduce-scatter.27
  1955.9 48.3 all-reduce.45
where the time goes:
time: 2070 us; the launch traced here: 2030 us
  local copies, waits for them, and re-layouts  1370 us (66%)
  blocking collectives  212 us (10%)
  other arithmetic  193 us (9%)
  matrix products  168 us (8%)
  starting transfers between devices  29.9 us (1%)
  waiting for transfers between devices  26.2 us (1%)
    unnamed x216, local copies, waits for them, and re-layouts  1080 us
    dynamic_update_slice x4, local copies, waits for them, and re-layouts, row_one_block(): lax.dynamic_update_slice_in_dim(d_full, d_scores.astype(jnp.float32), fir...  71.3 us
    unnamed x2, blocking collectives  59 us
    dot_general x8, matrix products, block_scores(): jnp.einsum('qhd,khd->hqk', query_blk, key_row, preferred_element_type=jnp...  45.4 us
  transfers between devices with their start and end apart: 26, of which 2 were waited for; matrix products, arithmetic and copies ran while one was open for 83% of the time, Pallas kernels for 0%

commit v1 on v0

v1 whole, which is shorter than its diff:
```python
import functools
import jax, jax.numpy as jnp
from jax import lax
from jax.experimental import pallas as pl
from jax.experimental.pallas import tpu as pltpu
DH=64
NEG=-1e9
F32, BF16 = jnp.float32, jnp.bfloat16


def dot_nt(a, b):
    return lax.dot_general(a, b, (((1,), (1,)), ((), ())), preferred_element_type=F32)


def dot_nn(a, b):
    return lax.dot_general(a, b, (((1,), (0,)), ((), ())), preferred_element_type=F32)


def fill_strips(rev_ref, strip_ref, heads, blk, nblk):
    for head in range(heads):
        for part in range(2 * nblk - 1):
            low = (2 * nblk - 2 - part) * blk
            segment = jnp.broadcast_to(rev_ref[head : head + 1, low : low + 2 * blk], (blk, 2 * blk))
            turned = pltpu.roll(segment, 0, 1, stride=1, stride_axis=0)
            strip_ref[head, part * blk : (part + 1) * blk, :] = turned[:, blk:]


def key_side(key, ok_col):
    rows = key.shape[0]
    lane = lax.broadcasted_iota(jnp.int32, (rows, DH), 1)
    extra = jnp.where(lane == 0, ok_col, 0.0).astype(BF16)
    return jnp.concatenate([key, extra], axis=1)


def query_side(query):
    rows = query.shape[0]
    lane = lax.broadcasted_iota(jnp.int32, (rows, DH), 1)
    return jnp.concatenate([query, jnp.where(lane == 0, 1.0, 0.0).astype(BF16)], axis=1)


def mask_column(place_ref, limit, blk, nblk):
    cols = []
    for b in range(nblk):
        at = place_ref[b] * blk + lax.broadcasted_iota(jnp.int32, (blk, DH), 0)
        cols.append(jnp.where(2 * at < limit, 0.0, NEG))
    return jnp.concatenate(cols, axis=0)


def attend_kernel(heads, blk, nblk, place_ref, len_ref, qkv_ref, rev_ref, out_ref, log_ref, strip_ref, kaug_ref, qaug_ref, vt_ref):
    row = pl.program_id(0)

    @pl.when(row == 0)
    def _():
        fill_strips(rev_ref, strip_ref, heads, blk, nblk)

    ok_col = mask_column(place_ref, len_ref[row], blk, nblk)
    width = heads * DH
    for head in range(heads):
        at = head * DH
        qaug_ref[...] = query_side(qkv_ref[0, :, at : at + DH])
        kaug_ref[...] = key_side(qkv_ref[0, :, width + at : width + at + DH], ok_col)
        vt_ref[...] = qkv_ref[0, :, 2 * width + at : 2 * width + at + DH].T

        def one_block(qb, carry):
            q_at = pl.multiple_of(qb * blk, blk)
            q_place = place_ref[qb]
            query = qaug_ref[pl.ds(q_at, blk), :]
            parts = []
            for kb in range(nblk):
                m_at = pl.multiple_of((place_ref[kb] - q_place + nblk - 1) * blk, blk)
                parts.append(dot_nt(kaug_ref[kb * blk : (kb + 1) * blk, :], query) + strip_ref[head, pl.ds(m_at, blk), :])
            top = functools.reduce(jnp.maximum, [jnp.max(p, axis=0, keepdims=True) for p in parts])
            total = jnp.zeros((1, blk), F32)
            acc = jnp.zeros((DH, blk), F32)
            for kb in range(nblk):
                weight = jnp.exp(parts[kb] - top)
                total += jnp.sum(weight, axis=0, keepdims=True)
                acc += dot_nn(vt_ref[:, kb * blk : (kb + 1) * blk], weight.astype(BF16))
            o_at = pl.multiple_of(q_place * blk, blk)
            out_ref[0, pl.ds(o_at, blk), at : at + DH] = (acc / total).T.astype(BF16)
            log_ref[0, head, pl.ds(qb, 1), :] = top + jnp.log(total)
            return carry

        lax.fori_loop(0, nblk, one_block, 0)


def attend(place, row_len, qkv, rev, heads, nblk):
    rows, tokens = qkv.shape[:2]
    blk = tokens // nblk
    return pl.pallas_call(
        functools.partial(attend_kernel, heads, blk, nblk),
        grid_spec=pltpu.PrefetchScalarGridSpec(
            num_scalar_prefetch=2,
            grid=(rows,),
            in_specs=[
                pl.BlockSpec((1, tokens, 3 * heads * DH), lambda r, *_: (r, 0, 0)),
                pl.BlockSpec(rev.shape, lambda r, *_: (0, 0)),
            ],
            out_specs=[
                pl.BlockSpec((1, tokens, heads * DH), lambda r, *_: (r, 0, 0)),
                pl.BlockSpec((1, heads, nblk, blk), lambda r, *_: (r, 0, 0, 0)),
            ],
            scratch_shapes=[
                pltpu.VMEM((heads, (2 * nblk - 1) * blk, blk), F32),
                pltpu.VMEM((tokens, 2 * DH), BF16),
                pltpu.VMEM((tokens, 2 * DH), BF16),
                pltpu.VMEM((DH, tokens), BF16),
            ],
        ),
        out_shape=[
            jax.ShapeDtypeStruct((rows, tokens, heads * DH), BF16),
            jax.ShapeDtypeStruct((rows, heads, nblk, blk), F32),
        ],
        compiler_params=pltpu.CompilerParams(vmem_limit_bytes=48 << 20),
        cost_estimate=pl.CostEstimate(flops=16 * rows * heads * tokens * tokens * DH, bytes_accessed=rows * tokens * heads * DH * 8, transcendentals=rows * heads * tokens * tokens),
        name="attend",
    )(place, row_len, qkv, rev)


def attend_back_kernel(heads, blk, nblk, place_ref, len_ref, qkv_ref, out_ref, dout_ref, log_ref, rev_ref, dqkv_ref, drev_ref,
                       strip_ref, grads_ref, kaug_ref, qaug_ref, kt_ref, dk_ref, dv_ref):
    row = pl.program_id(0)

    @pl.when(row == 0)
    def _():
        fill_strips(rev_ref, strip_ref, heads, blk, nblk)
        grads_ref[...] = jnp.zeros_like(grads_ref)

    ok_col = mask_column(place_ref, len_ref[row], blk, nblk)
    width = heads * DH
    for head in range(heads):
        at = head * DH
        qaug_ref[...] = query_side(qkv_ref[0, :, at : at + DH])
        key = qkv_ref[0, :, width + at : width + at + DH]
        kaug_ref[...] = key_side(key, ok_col)
        kt_ref[...] = key.T
        dk_ref[...] = jnp.zeros_like(dk_ref)
        dv_ref[...] = jnp.zeros_like(dv_ref)

        def one_block(qb, carry):
            q_at = pl.multiple_of(qb * blk, blk)
            q_place = place_ref[qb]
            o_at = pl.multiple_of(q_place * blk, blk)
            query = qaug_ref[pl.ds(q_at, blk), :]
            dout = dout_ref[0, pl.ds(o_at, blk), at : at + DH]
            prod = dout.astype(F32) * out_ref[0, pl.ds(o_at, blk), at : at + DH].astype(F32)
            inner = jnp.sum(prod.T, axis=0, keepdims=True)
            log_row = log_ref[0, head, pl.ds(qb, 1), :]
            dqt = jnp.zeros((DH, blk), F32)
            for kb in range(nblk):
                here = slice(kb * blk, (kb + 1) * blk)
                m_at = pl.multiple_of((place_ref[kb] - q_place + nblk - 1) * blk, blk)
                score = dot_nt(kaug_ref[here, :], query) + strip_ref[head, pl.ds(m_at, blk), :]
                prob = jnp.exp(score - log_row)
                d_prob = dot_nt(qkv_ref[0, here, 2 * width + at : 2 * width + at + DH], dout)
                d_score = prob * (d_prob - inner)
                low = d_score.astype(BF16)
                grads_ref[head, pl.ds(m_at, blk), :] += d_score
                dv_ref[here, :] += dot_nn(prob.astype(BF16), dout)
                dk_ref[here, :] += dot_nn(low, query[:, :DH])
                dqt += dot_nn(kt_ref[:, here], low)
            dqkv_ref[0, pl.ds(q_at, blk), at : at + DH] = dqt.T.astype(BF16)
            return carry

        lax.fori_loop(0, nblk, one_block, 0)
        dqkv_ref[0, :, width + at : width + at + DH] = dk_ref[...].astype(BF16)
        dqkv_ref[0, :, 2 * width + at : 2 * width + at + DH] = dv_ref[...].astype(BF16)

    @pl.when(row == pl.num_programs(0) - 1)
    def _():
        flip = (
            lax.broadcasted_iota(jnp.int32, (blk, blk), 0) + lax.broadcasted_iota(jnp.int32, (blk, blk), 1) == blk - 1
        ).astype(F32).astype(BF16)
        drev_ref[...] = jnp.zeros_like(drev_ref)
        for head in range(heads):
            for part in range(2 * nblk - 1):
                grad = grads_ref[head, part * blk : (part + 1) * blk, :]
                high = grad.astype(BF16)
                rest = (grad - high.astype(F32)).astype(BF16)
                turned = dot_nn(flip, high) + dot_nn(flip, rest)
                wide = jnp.concatenate([jnp.zeros((blk, blk), F32), turned], axis=1)
                moved = pltpu.roll(wide, blk + 1, 1, stride=1, stride_axis=0)
                low = (2 * nblk - 2 - part) * blk
                drev_ref[head : head + 1, low : low + 2 * blk] += jnp.sum(moved, axis=0, keepdims=True)


def attend_back(place, row_len, qkv, out, dout, logs, rev, heads, nblk):
    rows, tokens = qkv.shape[:2]
    blk = tokens // nblk
    return pl.pallas_call(
        functools.partial(attend_back_kernel, heads, blk, nblk),
        grid_spec=pltpu.PrefetchScalarGridSpec(
            num_scalar_prefetch=2,
            grid=(rows,),
            in_specs=[
                pl.BlockSpec((1, tokens, 3 * heads * DH), lambda r, *_: (r, 0, 0)),
                pl.BlockSpec((1, tokens, heads * DH), lambda r, *_: (r, 0, 0)),
                pl.BlockSpec((1, tokens, heads * DH), lambda r, *_: (r, 0, 0)),
                pl.BlockSpec((1, heads, nblk, blk), lambda r, *_: (r, 0, 0, 0)),
                pl.BlockSpec(rev.shape, lambda r, *_: (0, 0)),
            ],
            out_specs=[
                pl.BlockSpec((1, tokens, 3 * heads * DH), lambda r, *_: (r, 0, 0)),
                pl.BlockSpec(rev.shape, lambda r, *_: (0, 0)),
            ],
            scratch_shapes=[
                pltpu.VMEM((heads, (2 * nblk - 1) * blk, blk), F32),
                pltpu.VMEM((heads, (2 * nblk - 1) * blk, blk), F32),
                pltpu.VMEM((tokens, 2 * DH), BF16),
                pltpu.VMEM((tokens, 2 * DH), BF16),
                pltpu.VMEM((DH, tokens), BF16),
                pltpu.VMEM((tokens, DH), F32),
                pltpu.VMEM((tokens, DH), F32),
            ],
        ),
        out_shape=[
            jax.ShapeDtypeStruct((rows, tokens, 3 * heads * DH), BF16),
            jax.ShapeDtypeStruct(rev.shape, F32),
        ],
        compiler_params=pltpu.CompilerParams(vmem_limit_bytes=56 << 20),
        cost_estimate=pl.CostEstimate(flops=40 * rows * heads * tokens * tokens * DH, bytes_accessed=rows * tokens * heads * DH * 16, transcendentals=rows * heads * tokens * tokens),
        name="attend_back",
    )(place, row_len, qkv, out, dout, logs, rev)


EPS = 1e-06
VOCAB = 259
P = jax.sharding.PartitionSpec


def extended_2(x, width):
    size, length = lax.axis_size("seq"), x.shape[1]
    up = [(i, i + 1) for i in range(size - 1)]
    down = [(j, i) for i, j in up]
    before = lax.ppermute(x[:, length - width :], "seq", up)
    after = lax.ppermute(x[:, :width], "seq", down)
    return jnp.concatenate([before, x, after], axis=1)


def rms_norm(hidden, gain_vec):
    factor = lax.rsqrt(jnp.mean(hidden * hidden, axis=-1, keepdims=True) + EPS)
    return hidden * factor * gain_vec


def geglu(gate_in, upward):
    return jax.nn.gelu(gate_in, approximate=True) * upward


def block_means(padded, offset, extent):
    places = offset + jnp.arange(extent, dtype=jnp.int32)
    results = []
    for block_len in range(1, 5):
        remain = places % block_len
        summed = 0.0
        for shift_at in range(1 - block_len, block_len):
            select = ((shift_at >= -remain) & (shift_at <= block_len - 1 - remain)).astype(F32)
            summed = summed + select[:, None] * padded[..., 3 + shift_at : 3 + shift_at + extent, :]
        results.append(summed / block_len)
    return results


def mix_blocks(padded, offset, extent, score_vec):
    averages = block_means(padded, offset, extent)
    scores = jnp.stack([jnp.sum(mean_b * score_vec, axis=-1) for mean_b in averages], axis=0)
    shares = jax.nn.softmax(scores, axis=0)
    pooled = sum((shares[which_b][..., None] * averages[which_b] for which_b in range(4)))
    dims_all = pooled.shape
    return jnp.mean(pooled.reshape(dims_all[:-2] + (dims_all[-2] // 2, 2, dims_all[-1])), axis=-2)


def front_part(extended, conv_vec, score_vec, offset, row_len):
    extent = extended.shape[1] - 8
    conv_out = sum(
        (conv_vec[tap_at] * extended[:, tap_at : tap_at + extent + 4] for tap_at in range(4))
    )
    places = offset - 2 + jnp.arange(extent + 4, dtype=jnp.int32)
    inside = (places[None, :] >= 0) & (places[None, :] < row_len[:, None])
    conv_out = conv_out * inside[:, :, None].astype(F32)
    padded = jnp.pad(conv_out, ((0, 0), (1, 1), (0, 0)))
    return mix_blocks(padded, offset, extent, score_vec)


def flip_with(x, axis, bit):
    return lax.ppermute(x, axis, [(i, i ^ bit) for i in range(lax.axis_size(axis))])


def bits_of(axis):
    bits, bit = [], 1
    while bit < lax.axis_size(axis):
        bits.append(bit)
        bit *= 2
    return bits[::-1]


def gather_blocks(x):
    blocks = [x]
    for bit in bits_of("seq"):
        blocks = blocks + [flip_with(block, "seq", bit) for block in blocks]
    return jnp.stack(blocks, axis=1)


def places_of(n):
    places = [0]
    bit = n // 2
    while bit:
        places = places + [p ^ bit for p in places]
        bit //= 2
    return places


def scatter_blocks(parts):
    for bit in bits_of("seq")[::-1]:
        half = len(parts) // 2
        got = [flip_with(part.astype(BF16), "seq", bit) for part in parts[half:]]
        parts = [mine.astype(F32) + other.astype(F32) for mine, other in zip(parts[:half], got)]
    return parts[0]


def gather_dp(x):
    me = lax.axis_index("dp")
    bits = bits_of("dp")
    for _ in bits:
        x = x[None]
    for at, bit in enumerate(bits):
        other = flip_with(x, "dp", bit)
        upper = (me & bit) != 0
        x = jnp.concatenate([jnp.where(upper, other, x), jnp.where(upper, x, other)], axis=at)
    return x.reshape((lax.axis_size("dp"),) + x.shape[len(bits) :])


def scatter_dp(x):
    me = lax.axis_index("dp")
    bits = bits_of("dp")[::-1]
    x = x.reshape((2,) * len(bits) + x.shape[1:])
    for bit in bits:
        axis = [b for b in bits[::-1]].index(bit)
        low, high = lax.index_in_dim(x, 0, axis), lax.index_in_dim(x, 1, axis)
        upper = (me & bit) != 0
        keep, send = jnp.where(upper, high, low), jnp.where(upper, low, high)
        x = keep.astype(F32) + flip_with(send.astype(BF16), "dp", bit).astype(F32)
    return x.reshape(x.shape[len(bits) :])


def sum_seq(x):
    for bit in bits_of("seq")[::-1]:
        x = x + flip_with(x, "seq", bit)
    return x


def on_device(
    byte_ids,
    lengths,
    deal_order,
    buckets,
    embedding,
    conv_w,
    score_w,
    gain_one,
    w_query,
    w_key,
    w_value,
    w_out,
    rel_bias,
    gain_two,
    w_gate,
    w_up,
    w_down,
    cotangent,
):
    n = lax.axis_size("seq")
    dp = lax.axis_size("dp")
    me = lax.axis_index("seq")
    rows_dev, extent = byte_ids.shape
    share, width = w_query.shape
    d_model = share * dp
    head_cols = width // n
    heads_dev = head_cols // DH
    ff_cols = w_gate.shape[1] // n
    down_rows = w_down.shape[0] // n
    tok = cotangent.shape[1]
    seq_len = tok * n
    place = jnp.array(places_of(n), jnp.int32) ^ me

    vocab = embedding.shape[0]
    front_pack = jnp.concatenate(
        [embedding, conv_w, score_w[None], gain_one[None], gain_two[None]], axis=0
    )
    front_all = gather_dp(front_pack).transpose(1, 0, 2).reshape(vocab + 7, d_model)
    emb_all = front_all[:vocab]
    conv_all = front_all[vocab : vocab + 4]
    score_all, gain_first, gain_second = (front_all[vocab + 4 + i] for i in range(3))

    def own_cols(weight):
        return lax.dynamic_slice_in_dim(weight, me * head_cols, head_cols, 1)

    qkv_pack = jnp.concatenate([own_cols(w_query), own_cols(w_key), own_cols(w_value)], axis=1)
    qkv_w = gather_dp(qkv_pack).reshape(d_model, 3 * head_cols)

    def own_ff(weight):
        return lax.dynamic_index_in_dim(weight.reshape(share, dp, n, down_rows), me, 2, keepdims=False).reshape(
            share, ff_cols
        )

    down_own = lax.dynamic_slice_in_dim(w_down, me * down_rows, down_rows, 0)
    pad_rows = max(share, down_rows)
    rest_pack = jnp.concatenate([own_ff(w_gate), own_ff(w_up), w_out], axis=1)
    rest_pack = jnp.pad(rest_pack, ((0, pad_rows - share), (0, 0)))
    rest_pack = jnp.concatenate([rest_pack, jnp.pad(down_own, ((0, pad_rows - down_rows), (0, 0)))], axis=1)
    rest_all = lax.all_gather(rest_pack, "dp", axis=0, tiled=False)
    gate_up_w = rest_all[:, :share, : 2 * ff_cols].reshape(d_model, 2 * ff_cols)
    out_w = rest_all[:, :share, 2 * ff_cols : 2 * ff_cols + width].reshape(d_model, width)
    down_w = rest_all[:, :down_rows, 2 * ff_cols + width :].reshape(ff_cols, width)

    offset = me * extent
    matches = deal_order[:, None] == jnp.arange(lengths.shape[0], dtype=jnp.int32)[None, :]
    row_len = jnp.sum(jnp.where(matches, lengths[None, :], 0), axis=1)
    places = offset + jnp.arange(extent, dtype=jnp.int32)
    live = (places[None, :] < row_len[:, None]).astype(BF16)[:, :, None]
    onehot_ids = (byte_ids[:, :, None] == jnp.arange(vocab, dtype=jnp.int32)).astype(BF16)
    masked = jnp.einsum("rtv,vd->rtd", onehot_ids, emb_all, preferred_element_type=F32).astype(BF16) * live
    extended = extended_2(masked, 4)

    def front_call(ext_in, conv_in, score_in):
        return front_part(ext_in, conv_in, score_in, offset, row_len)

    h_zero, front_back = jax.vjp(
        front_call, extended.astype(F32), conv_all.astype(F32), score_all.astype(F32)
    )
    normed_one, norm_one_back = jax.vjp(rms_norm, h_zero, gain_first.astype(F32))
    low_one = gather_blocks(normed_one.astype(BF16)).reshape(rows_dev, seq_len, d_model)
    qkv = jnp.einsum("rtd,de->rte", low_one, qkv_w, preferred_element_type=F32).astype(BF16)

    first_head = me * heads_dev
    bias_loc = lax.dynamic_slice_in_dim(rel_bias, first_head, heads_dev, 1)
    offsets = jnp.concatenate([jnp.full((1,), -1, jnp.int32), buckets[::-1]])
    onehot = (offsets[None, :] == jnp.arange(rel_bias.shape[0], dtype=jnp.int32)[:, None]).astype(BF16)
    rev = jnp.einsum("nh,nx->hx", bias_loc, onehot, preferred_element_type=F32)

    attended_heads, logs = attend(place, row_len, qkv, rev, heads_dev, n)
    attended = lax.all_to_all(attended_heads, "seq", split_axis=1, concat_axis=2, tiled=True)
    h_one = h_zero + jnp.dot(attended, out_w, preferred_element_type=F32)
    normed_two, norm_two_back = jax.vjp(rms_norm, h_one, gain_second.astype(F32))
    low_two = gather_blocks(normed_two.astype(BF16)).reshape(rows_dev, seq_len, d_model)
    cot_all = gather_blocks(cotangent).reshape(rows_dev, seq_len, d_model)
    gate_up = jnp.dot(low_two, gate_up_w, preferred_element_type=F32)
    mixed_ff, ff_back = jax.vjp(geglu, gate_up[..., :ff_cols], gate_up[..., ff_cols:])
    hidden = mixed_ff.astype(BF16)

    def blocks_of(x):
        x = x.reshape(rows_dev, n, tok, x.shape[-1])
        return [x[:, b] for b in range(n)]

    ff_out = scatter_blocks(blocks_of(jnp.dot(hidden, down_w, preferred_element_type=F32)))
    output = (h_one + ff_out).astype(BF16)
    grad_down = jnp.einsum("gtf,gtd->fd", hidden, cot_all, preferred_element_type=F32)
    d_hidden = jnp.einsum("gtd,fd->gtf", cot_all, down_w, preferred_element_type=F32)
    d_gate_f, d_up_f = ff_back(d_hidden)
    d_gate_up = jnp.concatenate([d_gate_f.astype(BF16), d_up_f.astype(BF16)], axis=-1)
    grad_gate_up = jnp.einsum("gtd,gtf->df", low_two, d_gate_up, preferred_element_type=F32)
    d_norm_two = scatter_blocks(
        blocks_of(jnp.einsum("gtf,df->gtd", d_gate_up, gate_up_w, preferred_element_type=F32))
    )
    d_h_norm, grad_gain_two = norm_two_back(d_norm_two)
    d_h_one = cotangent.astype(F32) + d_h_norm
    d_branch = d_h_one.astype(BF16)
    grad_out = jnp.einsum("gtd,gte->de", attended, d_branch, preferred_element_type=F32)
    d_attended = jnp.einsum("gte,de->gtd", d_branch, out_w, preferred_element_type=F32).astype(BF16)
    d_heads = lax.all_to_all(d_attended, "seq", split_axis=2, concat_axis=1, tiled=True)

    d_qkv, d_rev = attend_back(place, row_len, qkv, attended_heads, d_heads, logs, rev, heads_dev, n)
    grad_qkv = jnp.einsum("gtd,gte->de", low_one, d_qkv, preferred_element_type=F32)
    d_norm_one = scatter_blocks(
        blocks_of(jnp.einsum("gte,de->gtd", d_qkv, qkv_w, preferred_element_type=F32))
    )
    d_h_first, grad_gain_one = norm_one_back(d_norm_one)
    d_h_zero = d_h_one + d_h_first
    d_ext, grad_conv, grad_score = front_back(d_h_zero)
    rim_out = jnp.concatenate([d_ext[:, :4], d_ext[:, -4:]], axis=1)
    rim_in = extended_2(rim_out.astype(BF16), 4).astype(rim_out.dtype)
    d_masked = d_ext[:, 4:-4] + jnp.pad(rim_in[:, :4], ((0, 0), (0, extent - 4), (0, 0)))
    d_masked = d_masked + jnp.pad(rim_in[:, 12:], ((0, 0), (extent - 4, 0), (0, 0)))
    d_input = (d_masked * live.astype(F32)).astype(BF16)
    grad_emb = jnp.einsum("rtv,rtd->vd", onehot_ids, d_input, preferred_element_type=F32)

    d_rel_loc = jnp.einsum("nx,hx->nh", onehot.astype(F32), d_rev, precision=lax.Precision.HIGHEST)
    d_rel_full = lax.dynamic_update_slice_in_dim(
        jnp.zeros(rel_bias.shape, F32), d_rel_loc, first_head, 1
    )
    grad_rel_bias = lax.psum(d_rel_full, ("dp", "seq"))

    pad_ff = jnp.pad(grad_gate_up.astype(BF16).reshape(dp, share, 2 * ff_cols), ((0, 0), (0, pad_rows - share), (0, 0)))
    pad_down = jnp.pad(
        grad_down.astype(BF16).reshape(dp, down_rows, width), ((0, 0), (0, pad_rows - down_rows), (0, 0))
    )
    ff_sum = lax.psum_scatter(jnp.concatenate([pad_ff, pad_down], axis=2), "dp", scatter_dimension=0, tiled=False)

    late = jnp.concatenate(
        [grad_qkv.reshape(dp, share, 3 * head_cols), grad_out.reshape(dp, share, width)], axis=2
    )
    late_sum = scatter_dp(late)
    front_grads = jnp.concatenate(
        [grad_emb, grad_conv, grad_score[None], grad_gain_one[None], grad_gain_two[None]], axis=0
    )
    front_sum = sum_seq(scatter_dp(front_grads.reshape(vocab + 7, dp, share).transpose(1, 0, 2)))
    g_out = sum_seq(late_sum[:, 3 * head_cols :])

    own = jnp.concatenate(
        [
            late_sum[:, : 3 * head_cols].astype(BF16).reshape(-1),
            ff_sum[:share, : 2 * ff_cols].reshape(-1),
            ff_sum[:down_rows, 2 * ff_cols :].reshape(-1),
        ]
    )
    every = lax.all_gather(own, "seq", axis=0, tiled=False).astype(F32)
    cut = share * 3 * head_cols
    cut_two = cut + share * 2 * ff_cols
    g_qkv = every[:, :cut].reshape(n, share, 3, head_cols).transpose(2, 1, 0, 3).reshape(3, share, width)
    g_gu = (
        every[:, cut:cut_two].reshape(n, share, 2, dp, down_rows).transpose(2, 1, 3, 0, 4).reshape(2, share, n * ff_cols)
    )
    g_down = every[:, cut_two:].reshape(n * down_rows, width)
    return (
        output,
        d_input,
        front_sum[:vocab],
        front_sum[vocab : vocab + 4],
        front_sum[vocab + 4],
        front_sum[vocab + 5],
        g_qkv[0],
        g_qkv[1],
        g_qkv[2],
        g_out,
        grad_rel_bias,
        front_sum[vocab + 6],
        g_gu[0],
        g_gu[1],
        g_down,
    )


def solution(mesh):
    return jax.shard_map(
        on_device,
        mesh=mesh,
        in_specs=(
            P("dp", "seq"),
            P(),
            P("dp"),
            P(),
            P(None, "dp"),
            P(None, "dp"),
            P("dp"),
            P("dp"),
            P("dp", None),
            P("dp", None),
            P("dp", None),
            P("dp", None),
            P(),
            P("dp"),
            P("dp", None),
            P("dp", None),
            P("dp", None),
            P("dp", "seq", None),
        ),
        out_specs=(
            P("dp", "seq", None),
            P("dp", "seq", None),
            P(None, "dp"),
            P(None, "dp"),
            P("dp"),
            P("dp"),
            P("dp", None),
            P("dp", None),
            P("dp", None),
            P("dp", None),
            P(),
            P("dp"),
            P("dp", None),
            P("dp", None),
            P("dp", None),
        ),
        check_vma=False,
    )
```

time: 2070 us -> 572 us (0.28); the launches traced: 2030 us -> 567 us
  local copies, waits for them, and re-layouts: 1370 us -> 89.1 us
  blocking collectives: 212 us -> 42.7 us
  waiting for transfers between devices: 26.2 us -> 155 us
  matrix products: 168 us -> 43.1 us
  other arithmetic: 193 us -> 110 us
  Pallas kernels: 0 us -> 64.1 us
    unnamed x216 -> x179, local copies, waits for them, and re-layouts: 1080 us -> 19.7 us
    ppermute x4 -> x38, waiting for transfers between devices: 0.01 us -> 141 us  [the longest x34 139 us: flip_with(): lax.ppermute(x, axis, [(i, i ^ bit) for i in range(lax.axis_size(axis))])]
    dot_general x51 -> x16, matrix products: 168 us -> 43.1 us  [the longest x1 7.9 us: on_device(): jnp.einsum('gtd,gtf->df', low_two, d_gate_up, preferred_element_type=F32)]
    dynamic_update_slice x17 -> x1, local copies, waits for them, and re-layouts: 101 us -> 0.13 us  [on_device(): lax.dynamic_update_slice_in_dim(jnp.zeros(rel_bias.shape, F32), d_rel_loc...]
    pallas_call x0 -> x2, Pallas kernels: none -> 64.1 us  [the longest x1 38.9 us: attend_back(): pl.pallas_call(functools.partial(attend_back_kernel, heads, blk, nblk), g...]
    unnamed x2 -> x0, blocking collectives: 59 us -> none
    convert_element_type x45 -> x26, other arithmetic: 65.9 us -> 8.23 us  [the longest x3 4.09 us: scatter_blocks(): got = [flip_with(part.astype(BF16), 'seq', bit) for part in parts[half:]]]
    all_to_all x3 -> x0, blocking collectives: 51 us -> none  [the longest x1 17.2 us: on_device(): lax.all_to_all(d_query_h, 'seq', split_axis=1, concat_axis=2, tiled=True)]
  transfers between devices with their start and end apart: 26 -> 43, of which waited for: 2 -> 17; matrix products, arithmetic and copies ran while one was open for 83% -> 30% of each run, Pallas kernels for 0% -> 4%
where the time goes in v1:
time: 572 us; the launch traced here: 567 us
  waiting for transfers between devices  155 us (27%)
  other arithmetic  110 us (19%)
  local copies, waits for them, and re-layouts  89.1 us (16%)
  Pallas kernels  64.1 us (11%)
  starting transfers between devices  47.2 us (8%)
  matrix products  43.1 us (8%)
  blocking collectives  42.7 us (7%)
  between operations  16.2 us (3%)
    ppermute x34, waiting for transfers between devices, flip_with(): lax.ppermute(x, axis, [(i, i ^ bit) for i in range(lax.axis_size(axis))])  139 us
    psum x1, blocking collectives, on_device(): grad_rel_bias = lax.psum(d_rel_full, ('dp', 'seq'))  42.7 us
    pallas_call x1, Pallas kernels, attend_back(): pl.pallas_call(functools.partial(attend_back_kernel, heads, blk, nblk), g...  38.9 us
    ppermute x34, starting transfers between devices, flip_with(): lax.ppermute(x, axis, [(i, i ^ bit) for i in range(lax.axis_size(axis))])  32.5 us
    pallas_call x1, Pallas kernels, attend(): pl.pallas_call(functools.partial(attend_kernel, heads, blk, nblk), grid_s...  25.2 us
    mul x10, other arithmetic, block_means(): select[:, None] * padded[..., 3 + shift_at:3 + shift_at + extent, :]  22.5 us
    unnamed x179, local copies, waits for them, and re-layouts  19.7 us
    all_to_all x1, waiting for transfers between devices, on_device(): lax.all_to_all(attended_heads, 'seq', split_axis=1, concat_axis=2, tiled=...  12.9 us
  transfers between devices with their start and end apart: 43, of which 17 were waited for; matrix products, arithmetic and copies ran while one was open for 30% of the time, Pallas kernels for 4%

profile of v1, /device:TPU:0, one launch (start us, length us, event | category | flops | bytes accessed | tf_op | source)
XLA Modules:
  0.0 566.8 jit_solution(7932969264690977780)
XLA Ops:
  29.4 10.9 %collective-permute-done.2 = bf16[2,2,1,266,96]{4,3,2,1,0:T(8,128)(2,1)S(1)} collective-permute-done((bf16[2,2,1,266,96]{4,3,2,1,0:T(8,128)(2,1)S(1)}, bf16[2,2,1,266,96]{4,3,2,1,0:T(8,128)(2,1)S(1)}, u32[]{:S(2)}, u32[]{:S(2)}) %collective-permute-start.2) | collective-permute-done | bytes 204320 | tf_op jit(solution)/shard_map/ppermute | solution.py:284
  54.2 6.3 %multiply_reduce_fusion.14 = (f32[2,512]{1,0:T(2,128)S(1)}, f32[2,512,768]{2,1,0:T(8,128)}, f32[2,512]{1,0:T(2,128)S(1)}, f32[2,512,768]{2,1,0:T(8,128)}) fusion(f32[768]{0:T(1024)S(1)} %get-tuple-element.210, f32[2,516,768]{2,1,0:T(8,128)S(1)} %add_multiply_fusion, f32[512]{0:T(512)S(1)} %get-tuple-element.239, f32[512]{0:T(512)S(1)} %get-tuple-element.238, ...), kind=kLoop, calls=%fused_computation.57 | loop fusion | flops 14153728 | bytes 22050816 | tf_op jit(solution)/shard_map/jvp()/reduce_sum | solution.py:264
  70.6 5.6 reduce_sum.240
  80.1 15.5 %collective-permute-done.9 = bf16[2,1,1,96,576]{4,3,2,1,0:T(8,128)(2,1)S(1)} collective-permute-done((bf16[2,1,1,96,576]{4,3,2,1,0:T(8,128)(2,1)S(1)}, bf16[2,1,1,96,576]{4,3,2,1,0:T(8,128)(2,1)S(1)}, u32[]{:S(2)}, u32[]{:S(2)}) %collective-permute-start.9) | collective-permute-done | bytes 221216 | tf_op jit(solution)/shard_map/ppermute | solution.py:284
  97.4 11.5 %collective-permute-done.10 = bf16[2,2,1,96,576]{4,3,2,1,0:T(8,128)(2,1)S(1)} collective-permute-done((bf16[2,2,1,96,576]{4,3,2,1,0:T(8,128)(2,1)S(1)}, bf16[2,2,1,96,576]{4,3,2,1,0:T(8,128)(2,1)S(1)}, u32[]{:S(2)}, u32[]{:S(2)}) %collective-permute-start.10) | collective-permute-done | bytes 442400 | tf_op jit(solution)/shard_map/ppermute | solution.py:284
  114.6 25.2 %attend.1 = (bf16[2,1024,192]{2,1,0:T(8,128)(2,1)S(1)}, f32[2,3,4,256]{3,2,1,0:T(4,128)S(1)}) custom-call(s32[4]{0:T(128)S(1)} %broadcast_xor_fusion.place_ref, s32[2]{0:T(128)S(1)} %fusion.67.len_ref, bf16[2,1024,576]{2,1,0:T(8,128)(2,1)S(1)} %convolution_convert_fusion.qkv_ref, f32[3,2048]{1,0:T(4,128)S(1)} %fusion.55.rev_ref), custom_call_target="tpu_custom_call" | custom-call | flops 6442450944 | bytes 3145728 | tf_op jit(solution)/shard_map/attend/pallas_call | solution.py:90
  149.1 12.9 %all-to-all-done = bf16[2,1024,192]{2,0,1:T(2,128)(2,1)} async-done(((bf16[2,1024,192]{2,0,1:T(2,128)(2,1)}), bf16[2,1024,192]{2,0,1:T(2,128)(2,1)}, u32[]{:S(2)}, u32[]{:S(2)}) %all-to-all-start) | async-done | bytes 786464 | tf_op jit(solution)/shard_map/all_to_all | solution.py:440
  169.7 9.0 %collective-permute-done.17 = bf16[2,256,768]{2,1,0:T(8,128)(2,1)} collective-permute-done((bf16[2,256,768]{2,1,0:T(8,128)(2,1)}, bf16[2,256,768]{2,1,0:T(8,128)(2,1)}, u32[]{:S(2)}, u32[]{:S(2)}) %collective-permute-start.17) | collective-permute-done | bytes 786464 | tf_op jit(solution)/shard_map/ppermute | solution.py:284
  179.3 15.8 %collective-permute-done.11 = bf16[2,256,768]{2,1,0:T(8,128)(2,1)S(1)} collective-permute-done((bf16[2,256,768]{2,1,0:T(8,128)(2,1)S(1)}, bf16[2,256,768]{2,1,0:T(8,128)(2,1)S(1)}, u32[]{:S(2)}, u32[]{:S(2)}) %collective-permute-start.11) | collective-permute-done | bytes 786464 | tf_op jit(solution)/shard_map/ppermute | solution.py:284
  232.5 11.7 %collective-permute-done.22 = bf16[2,256,768]{2,1,0:T(8,128)(2,1)} collective-permute-done((bf16[2,256,768]{2,1,0:T(8,128)(2,1)}, bf16[2,256,768]{2,1,0:T(8,128)(2,1)}, u32[]{:S(2)}, u32[]{:S(2)}) %collective-permute-start.22) | collective-permute-done | bytes 786464 | tf_op jit(solution)/shard_map/ppermute | solution.py:284
  247.0 13.1 %collective-permute-done.16 = bf16[2,256,768]{2,1,0:T(8,128)(2,1)} collective-permute-done((bf16[2,256,768]{2,1,0:T(8,128)(2,1)}, bf16[2,256,768]{2,1,0:T(8,128)(2,1)}, u32[]{:S(2)}, u32[]{:S(2)}) %collective-permute-start.16) | collective-permute-done | bytes 786464 | tf_op jit(solution)/shard_map/ppermute | solution.py:284
  273.2 7.9 %bitcast_convert_fusion = bf16[768,1024]{1,0:T(8,128)(2,1)} fusion(bf16[2,1024,768]{2,1,0:T(8,128)(2,1)} %bitcast.274, bf16[2,1024,512]{2,1,0:T(8,128)(2,1)} %copy-done.45, bf16[2,1024,512]{2,1,0:T(8,128)(2,1)} %copy-done.44), kind=kOutput, calls=%fused_computation.39 | convolution fusion | flops 3230400512 | bytes 8912896 | tf_op jit(solution)/shard_map/gtd,gtf->df/dot_general | solution.py:459
  286.9 38.9 %attend_back.1 = (bf16[2,1024,576]{2,1,0:T(8,128)(2,1)}, f32[3,2048]{1,0:T(4,128)}) custom-call(s32[4]{0:T(128)} %copy-done.4, s32[2]{0:T(128)} %copy-done.3, bf16[2,1024,576]{2,1,0:T(8,128)(2,1)} %copy-done.6, bf16[2,1024,192]{2,1,0:T(8,128)(2,1)} %copy-done.2, bf16[2,1024,192]{2,1,0:T(8,128)(2,1)} %bitcast.285, f32[2,3,4,256]{3,2,1,0:T(4,128)} %copy-done.7, ...), custom_call_target="tpu_custom_call" | custom-call | flops 16106127360 | bytes 6291456 | tf_op jit(solution)/shard_map/attend_back/pallas_call | solution.py:190
  339.9 17.0 %collective-permute-done.33 = bf16[2,2,1,96,1344]{4,3,2,1,0:T(8,128)(2,1)S(1)} collective-permute-done((bf16[2,2,1,96,1344]{4,3,2,1,0:T(8,128)(2,1)S(1)}, bf16[2,2,1,96,1344]{4,3,2,1,0:T(8,128)(2,1)S(1)}, u32[]{:S(2)}, u32[]{:S(2)}) %collective-permute-start.33) | collective-permute-done | bytes 1032224 | tf_op jit(solution)/shard_map/ppermute | solution.py:284
  365.0 15.7 %collective-permute-done.34 = bf16[2,1,1,96,1344]{4,3,2,1,0:T(8,128)(2,1)} collective-permute-done((bf16[2,1,1,96,1344]{4,3,2,1,0:T(8,128)(2,1)}, bf16[2,1,1,96,1344]{4,3,2,1,0:T(8,128)(2,1)}, u32[]{:S(2)}, u32[]{:S(2)}) %collective-permute-start.34) | collective-permute-done | bytes 516128 | tf_op jit(solution)/shard_map/ppermute | solution.py:284
  390.6 5.6 reshape.616
  396.4 5.7 %multiply_reduce_fusion.11 = (f32[2,512]{1,0:T(2,128)S(1)}, f32[2,512]{1,0:T(2,128)S(1)}, f32[2,512]{1,0:T(2,128)S(1)}, f32[2,512]{1,0:T(2,128)S(1)}) fusion(f32[2,512,768]{2,1,0:T(8,128)} %reshape.616, f32[2,512,768]{2,1,0:T(8,128)} %copy-done.12, f32[2,516,768]{2,1,0:T(8,128)S(1)} %copy-done.9, f32[2,512,768]{2,1,0:T(8,128)} %get-tuple-element.118, ...), kind=kLoop, calls=%fused_computation.51 | loop fusion | flops 8646656 | bytes 15745024 | tf_op jit(solution)/shard_map/transpose(jvp())/reduce_sum | solution.py:266
  402.3 12.8 %broadcast_multiply_fusion.15 = (f32[2,512,768]{2,1,0:T(8,128)}, f32[2,512,768]{2,1,0:T(8,128)}, f32[2,512,768]{2,1,0:T(8,128)}, f32[2,512,768]{2,1,0:T(8,128)},...) fusion(f32[512]{0:T(512)S(1)} %copy-done.70, ...), kind=kLoop, calls=%fused_computation.123 | loop fusion | flops 14155776 | bytes 40938496 | tf_op jit(solution)/shard_map/transpose(jvp())/mul | solution.py:257
  415.1 5.5 fusion.23
  420.7 10.9 %pad_add_fusion.7 = f32[2,518,768]{2,1,0:T(8,128)S(1)} fusion(f32[2,512,768]{2,1,0:T(8,128)} %get-tuple-element.150, f32[2,512,768]{2,1,0:T(8,128)} %get-tuple-element.151, f32[2,512,768]{2,1,0:T(8,128)} %get-tuple-element.152, f32[2,512,768]{2,1,0:T(8,128)} %get-tuple-element.139, f32[2,512,768]{2,1,0:T(8,128)} %get-tuple-element.138, ...), kind=kLoop, calls=%fused_computation.30 | loop fusion | flops 7160832 | bytes 34639872 | tf_op jit(solution)/shard_map/transpose(jvp())/add_any | solution.py:257
  431.9 6.6 %multiply_reduce_fusion.3 = (f32[768]{0:T(1024)S(1)}, f32[768]{0:T(1024)S(1)}, f32[768]{0:T(1024)S(1)}, f32[768]{0:T(1024)S(1)}, f32[2,516,768]{2,1,0:T(8,128)S(1)}) fusion(f32[2,520,768]{2,1,0:T(8,128)S(1)} %copy-done.11, f32[2,516]{1,0:T(2,128)S(1)} %copy-done.50, f32[2,512,768]{2,1,0:T(8,128)} %get-tuple-element.153, ...), kind=kLoop, calls=%fused_computation.28 | loop fusion | flops 11885568 | bytes 37912608 | tf_op jit(solution)/shard_map/transpose(jvp())/reduce_sum | solution.py:274
  460.5 6.1 %collective-permute-done.28 = bf16[2,2,1,266,96]{4,3,2,1,0:T(8,128)(2,1)S(1)} collective-permute-done((bf16[2,2,1,266,96]{4,3,2,1,0:T(8,128)(2,1)S(1)}, bf16[2,2,1,266,96]{4,3,2,1,0:T(8,128)(2,1)S(1)}, u32[]{:S(2)}, u32[]{:S(2)}) %collective-permute-start.28) | collective-permute-done | bytes 204320 | tf_op jit(solution)/shard_map/ppermute | solution.py:284
  481.2 5.5 collective-permute-start.32
  487.3 42.7 %psum.7 = f32[32,12]{0,1:T(8,128)} all-reduce(f32[32,12]{0,1:T(8,128)S(1)} %dynamic_update_slice.3), channel_id=1, replica_groups=mesh['dp'=8,'seq'=4] {'dp','seq'}, use_global_device_ids=true, to_apply=%region_27.28 | all-reduce | flops 384 | bytes 3072 | tf_op jit(solution)/shard_map/psum | solution.py:489
  (452 shorter events, 232.1 us)
Async XLA Ops:
  7.2 159.7 %all-gather.5.cloned.1.call-start = ((), (), s32[]{:S(2)}) async-start(), calls=%async_computation.4 | async-start | bytes 4423680 | tf_op jit(solution)/shard_map/all_gather | solution.py:409
  15.8 63.2 %collective-permute-start.8 = (bf16[1,1,1,96,576]{4,3,2,1,0:T(8,128)(2,1)S(1)}, bf16[1,1,1,96,576]{4,3,2,1,0:T(8,128)(2,1)S(1)}, u32[]{:S(2)}, u32[]{:S(2)}) collective-permute-start(bf16[1,1,1,96,576]{4,3,2,1,0:T(8,128)(2,1)S(1)} %maximum_bitcast_fusion), channel_id=1, source_target_pairs={{0,16},{4,20},{8,24},{12,28},{16,0},{20,4},{24,8},{28,12},{1,17},{... | collective-permute-start | bytes 331784 | tf_op jit(solution)/shard_map/ppermute | solution.py:284
  76.7 19.8 %collective-permute-start.5 = (bf16[2,256,768]{2,1,0:T(8,128)(2,1)S(1)}, bf16[2,256,768]{2,1,0:T(8,128)(2,1)S(1)}, u32[]{:S(2)}, u32[]{:S(2)}) collective-permute-start(bf16[2,256,768]{2,1,0:T(8,128)(2,1)S(1)} %multiply_convert_fusion.3), channel_id=1, source_target_pairs={{0,2},{1,3},{2,0},{3,1},{4,6},{5,7},{6,4},{7,5},{8,10},{9,11},{10,... | collective-permute-start | bytes 2359304 | tf_op jit(solution)/shard_map/ppermute | solution.py:284
  79.2 16.5 %collective-permute-start.9 = (bf16[2,1,1,96,576]{4,3,2,1,0:T(8,128)(2,1)S(1)}, bf16[2,1,1,96,576]{4,3,2,1,0:T(8,128)(2,1)S(1)}, u32[]{:S(2)}, u32[]{:S(2)}) collective-permute-start(bf16[2,1,1,96,576]{4,3,2,1,0:T(8,128)(2,1)S(1)} %pad_maximum_fusion.10), channel_id=1, source_target_pairs={{0,8},{4,12},{8,0},{12,4},{16,24},{20,28},{24,16},{28,20},{1,9},{5... | collective-permute-start | bytes 663560 | tf_op jit(solution)/shard_map/ppermute | solution.py:284
  142.4 19.5 %all-to-all-start = ((bf16[2,1024,192]{2,0,1:T(2,128)(2,1)}), bf16[2,1024,192]{2,0,1:T(2,128)(2,1)}, u32[]{:S(2)}, u32[]{:S(2)}) async-start(bf16[2,1024,192]{2,0,1:T(2,128)(2,1)} %copy.226), calls=%async_computation | async-start | bytes 2097152 | tf_op jit(solution)/shard_map/all_to_all | solution.py:440
  146.9 31.8 %collective-permute-start.17 = (bf16[2,256,768]{2,1,0:T(8,128)(2,1)}, bf16[2,256,768]{2,1,0:T(8,128)(2,1)}, u32[]{:S(2)}, u32[]{:S(2)}) collective-permute-start(bf16[2,256,768]{2,1,0:T(8,128)(2,1)} %param.36), channel_id=1, source_target_pairs={{0,2},{1,3},{2,0},{3,1},{4,6},{5,7},{6,4},{7,5},{8,10},{9,11},{10,... | collective-permute-start | bytes 2359304 | tf_op jit(solution)/shard_map/ppermute | solution.py:284
  169.6 25.5 %collective-permute-start.11 = (bf16[2,256,768]{2,1,0:T(8,128)(2,1)S(1)}, bf16[2,256,768]{2,1,0:T(8,128)(2,1)S(1)}, u32[]{:S(2)}, u32[]{:S(2)}) collective-permute-start(bf16[2,256,768]{2,1,0:T(8,128)(2,1)S(1)} %multiply_convert_fusion.2), channel_id=1, source_target_pairs={{0,2},{1,3},{2,0},{3,1},{4,6},{5,7},{6,4},{7,5},{8,10},{9,11},{10,... | collective-permute-start | bytes 2359304 | tf_op jit(solution)/shard_map/ppermute | solution.py:284
  169.7 25.9 %collective-permute-start.18 = (bf16[2,256,768]{2,1,0:T(8,128)(2,1)}, bf16[2,256,768]{2,1,0:T(8,128)(2,1)S(1)}, u32[]{:S(2)}, u32[]{:S(2)}) collective-permute-start(bf16[2,256,768]{2,1,0:T(8,128)(2,1)} %param.36), channel_id=1, source_target_pairs={{0,1},{1,0},{2,3},{3,2},{4,5},{5,4},{6,7},{7,6},{8,9},{9,8},{10,11... | collective-permute-start | bytes 2359304 | tf_op jit(solution)/shard_map/ppermute | solution.py:284
  178.8 16.9 %collective-permute-start.19 = (bf16[2,256,768]{2,1,0:T(8,128)(2,1)}, bf16[2,256,768]{2,1,0:T(8,128)(2,1)S(1)}, u32[]{:S(2)}, u32[]{:S(2)}) collective-permute-start(bf16[2,256,768]{2,1,0:T(8,128)(2,1)} %collective-permute-done.17), channel_id=1, source_target_pairs={{0,1},{1,0},{2,3},{3,2},{4,5},{5,4},{6,7},{7,6},{8,9},{9,8},{10,11... | collective-permute-start | bytes 2359304 | tf_op jit(solution)/shard_map/ppermute | solution.py:284
  178.8 21.1 %collective-permute-start.12 = (bf16[2,256,768]{2,1,0:T(8,128)(2,1)S(1)}, bf16[2,256,768]{2,1,0:T(8,128)(2,1)S(1)}, u32[]{:S(2)}, u32[]{:S(2)}) collective-permute-start(bf16[2,256,768]{2,1,0:T(8,128)(2,1)S(1)} %multiply_convert_fusion.2), channel_id=1, source_target_pairs={{0,1},{1,0},{2,3},{3,2},{4,5},{5,4},{6,7},{7,6},{8,9},{9,8},{10,11... | collective-permute-start | bytes 2359304 | tf_op jit(solution)/shard_map/ppermute | solution.py:284
  223.5 20.7 %collective-permute-start.22 = (bf16[2,256,768]{2,1,0:T(8,128)(2,1)}, bf16[2,256,768]{2,1,0:T(8,128)(2,1)}, u32[]{:S(2)}, u32[]{:S(2)}) collective-permute-start(bf16[2,256,768]{2,1,0:T(8,128)(2,1)} %fusion.35), channel_id=1, source_target_pairs={{0,2},{1,3},{2,0},{3,1},{4,6},{5,7},{6,4},{7,5},{8,10},{9,11},{10,... | collective-permute-start | bytes 2359304 | tf_op jit(solution)/shard_map/ppermute | solution.py:284
  225.0 22.0 %collective-permute-start.14 = (bf16[2,256,768]{2,1,0:T(8,128)(2,1)}, bf16[2,256,768]{2,1,0:T(8,128)(2,1)}, u32[]{:S(2)}, u32[]{:S(2)}) collective-permute-start(bf16[2,256,768]{2,1,0:T(8,128)(2,1)} %get-tuple-element.160), channel_id=1, source_target_pairs={{0,1},{1,0},{2,3},{3,2},{4,5},{5,4},{6,7},{7,6},{8,9},{9,8},{10,11... | collective-permute-start | bytes 2359304 | tf_op jit(solution)/shard_map/ppermute | solution.py:284
  226.1 34.0 %collective-permute-start.16 = (bf16[2,256,768]{2,1,0:T(8,128)(2,1)}, bf16[2,256,768]{2,1,0:T(8,128)(2,1)}, u32[]{:S(2)}, u32[]{:S(2)}) collective-permute-start(bf16[2,256,768]{2,1,0:T(8,128)(2,1)} %fusion.39), channel_id=1, source_target_pairs={{0,2},{1,3},{2,0},{3,1},{4,6},{5,7},{6,4},{7,5},{8,10},{9,11},{10,... | collective-permute-start | bytes 2359304 | tf_op jit(solution)/shard_map/ppermute | solution.py:284
  268.5 15.9 %all-to-all-start.1 = ((bf16[2,256,768]{1,0,2:T(2,128)(2,1)}), bf16[2,256,768]{1,0,2:T(2,128)(2,1)}, u32[]{:S(2)}, u32[]{:S(2)}) async-start(bf16[2,256,768]{1,0,2:T(2,128)(2,1)} %copy.244), calls=%async_computation.1 | async-start | bytes 1572864 | tf_op jit(solution)/shard_map/all_to_all | solution.py:468
  272.7 184.4 %reduce-scatter.2.cloned.1.call-start = ((), (), s32[]{:S(2)}) async-start(), calls=%async_computation.3 | async-start | bytes 3096576 | tf_op jit(solution)/shard_map/reduce_scatter | solution.py:495
  331.4 25.5 %collective-permute-start.33 = (bf16[2,2,1,96,1344]{4,3,2,1,0:T(8,128)(2,1)S(1)}, bf16[2,2,1,96,1344]{4,3,2,1,0:T(8,128)(2,1)S(1)}, u32[]{:S(2)}, u32[]{:S(2)}) collective-permute-start(bf16[2,2,1,96,1344]{4,3,2,1,0:T(8,128)(2,1)S(1)} %select_convert_fusion), channel_id=1, source_target_pairs={{0,4},{4,0},{8,12},{12,8},{16,20},{20,16},{24,28},{28,24},{1,5},{5... | collective-permute-start | bytes 3096584 | tf_op jit(solution)/shard_map/ppermute | solution.py:284
  339.9 21.7 %collective-permute-start.24 = (bf16[2,256,768]{2,1,0:T(8,128)(2,1)S(1)}, bf16[2,256,768]{2,1,0:T(8,128)(2,1)}, u32[]{:S(2)}, u32[]{:S(2)}) collective-permute-start(bf16[2,256,768]{2,1,0:T(8,128)(2,1)S(1)} %get-tuple-element.157), channel_id=1, source_target_pairs={{0,1},{1,0},{2,3},{3,2},{4,5},{5,4},{6,7},{7,6},{8,9},{9,8},{10,11... | collective-permute-start | bytes 2359304 | tf_op jit(solution)/shard_map/ppermute | solution.py:284
  359.5 21.1 %collective-permute-start.34 = (bf16[2,1,1,96,1344]{4,3,2,1,0:T(8,128)(2,1)}, bf16[2,1,1,96,1344]{4,3,2,1,0:T(8,128)(2,1)}, u32[]{:S(2)}, u32[]{:S(2)}) collective-permute-start(bf16[2,1,1,96,1344]{4,3,2,1,0:T(8,128)(2,1)} %select_convert_fusion.1), channel_id=1, source_target_pairs={{0,8},{4,12},{8,0},{12,4},{16,24},{20,28},{24,16},{28,20},{1,9},{5... | collective-permute-start | bytes 1548296 | tf_op jit(solution)/shard_map/ppermute | solution.py:284
  361.4 171.1 %all-gather.7.cloned.1.call-start = ((), (), s32[]{:S(2)}) async-start(), calls=%async_computation.5 | async-start | bytes 2027520 | tf_op jit(solution)/shard_map/all_gather | solution.py:514
  361.5 22.1 %collective-permute-start.23 = (bf16[2,256,768]{2,1,0:T(8,128)(2,1)S(1)}, bf16[2,256,768]{2,1,0:T(8,128)(2,1)S(1)}, u32[]{:S(2)}, u32[]{:S(2)}) collective-permute-start(bf16[2,256,768]{2,1,0:T(8,128)(2,1)S(1)} %get-tuple-element.156), channel_id=1, source_target_pairs={{0,1},{1,0},{2,3},{3,2},{4,5},{5,4},{6,7},{7,6},{8,9},{9,8},{10,11... | collective-permute-start | bytes 2359304 | tf_op jit(solution)/shard_map/ppermute | solution.py:284
  363.5 20.1 %collective-permute-start.25 = (bf16[2,256,768]{2,1,0:T(8,128)(2,1)S(1)}, bf16[2,256,768]{2,1,0:T(8,128)(2,1)S(1)}, u32[]{:S(2)}, u32[]{:S(2)}) collective-permute-start(bf16[2,256,768]{2,1,0:T(8,128)(2,1)S(1)} %fusion.31), channel_id=1, source_target_pairs={{0,2},{1,3},{2,0},{3,1},{4,6},{5,7},{6,4},{7,5},{8,10},{9,11},{10,... | collective-permute-start | bytes 2359304 | tf_op jit(solution)/shard_map/ppermute | solution.py:284
  383.6 72.8 %collective-permute-start.35 = (bf16[1,1,1,96,1344]{4,3,2,1,0:T(8,128)(2,1)}, bf16[1,1,1,96,1344]{4,3,2,1,0:T(8,128)(2,1)S(1)}, u32[]{:S(2)}, u32[]{:S(2)}) collective-permute-start(bf16[1,1,1,96,1344]{4,3,2,1,0:T(8,128)(2,1)} %select_convert_fusion.3), channel_id=1, source_target_pairs={{0,16},{4,20},{8,24},{12,28},{16,0},{20,4},{24,8},{28,12},{1,17},{... | collective-permute-start | bytes 774152 | tf_op jit(solution)/shard_map/ppermute | solution.py:284
  481.2 48.8 %collective-permute-start.32 = (f32[266,96]{1,0:T(8,128)S(1)}, f32[266,96]{1,0:T(8,128)S(1)}, u32[]{:S(2)}, u32[]{:S(2)}) collective-permute-start(f32[266,96]{1,0:T(8,128)S(1)} %add.433), channel_id=1, source_target_pairs={{0,2},{1,3},{2,0},{3,1},{4,6},{5,7},{6,4},{7,5},{8,10},{9,11},{10,... | collective-permute-start | bytes 306440 | tf_op jit(solution)/shard_map/ppermute | solution.py:284
  486.8 44.9 %collective-permute-start.37 = (f32[96,768]{1,0:T(8,128)S(1)}, f32[96,768]{1,0:T(8,128)S(1)}, u32[]{:S(2)}, u32[]{:S(2)}) collective-permute-start(f32[96,768]{1,0:T(8,128)S(1)} %slice_add_fusion.1), channel_id=1, source_target_pairs={{0,2},{1,3},{2,0},{3,1},{4,6},{5,7},{6,4},{7,5},{8,10},{9,11},{10,... | collective-permute-start | bytes 884744 | tf_op jit(solution)/shard_map/ppermute | solution.py:284
  (103 other events, 1053.3 us)
Sparse Core Ops, SparseCore 0:
  19.7 76.0 all-gather.4
  361.5 82.4 reduce-scatter.1
  460.0 23.8 all-gather.6

commit v2 on v1

v2 whole, which is shorter than its diff:
```python
import functools
import jax, jax.numpy as jnp
from jax import lax
from jax.experimental import pallas as pl
from jax.experimental.pallas import tpu as pltpu
DH=64
NEG=-1e9
F32, BF16 = jnp.float32, jnp.bfloat16


def dot_nt(a, b):
    return lax.dot_general(a, b, (((1,), (1,)), ((), ())), preferred_element_type=F32)


def dot_nn(a, b):
    return lax.dot_general(a, b, (((1,), (0,)), ((), ())), preferred_element_type=F32)


def tile_at(place_ref, kb, qb, nblk):
    return jnp.clip(place_ref[kb] - place_ref[qb], -2, 2) + 2


def strip_kernel(nblk, rev_ref, strip_ref):
    heads, _, blk = strip_ref.shape
    for head in range(heads):
        for part in range(5):
            low = (nblk + 1 - part) * blk
            here = slice(part * blk, (part + 1) * blk)
            if part in (0, 4):
                strip_ref[head, here, :] = jnp.broadcast_to(rev_ref[head : head + 1, low + blk : low + blk + 1], (blk, blk))
                continue
            segment = jnp.broadcast_to(rev_ref[head : head + 1, low : low + 2 * blk], (blk, 2 * blk))
            strip_ref[head, here, :] = pltpu.roll(segment, 0, 1, stride=1, stride_axis=0)[:, blk:]


def bias_strips(rev, nblk):
    heads, width = rev.shape
    blk = width // (2 * nblk)
    return pl.pallas_call(
        functools.partial(strip_kernel, nblk),
        out_shape=jax.ShapeDtypeStruct((heads, 5 * blk, blk), F32),
        compiler_params=pltpu.CompilerParams(vmem_limit_bytes=32 << 20),
        name="strips",
    )(rev)


def key_side(key, ok_col):
    rows = key.shape[0]
    lane = lax.broadcasted_iota(jnp.int32, (rows, DH), 1)
    extra = jnp.where(lane == 0, ok_col, 0.0).astype(BF16)
    return jnp.concatenate([key, extra], axis=1)


def query_side(query):
    rows = query.shape[0]
    lane = lax.broadcasted_iota(jnp.int32, (rows, DH), 1)
    return jnp.concatenate([query, jnp.where(lane == 0, 1.0, 0.0).astype(BF16)], axis=1)


def mask_column(place_ref, limit, blk, nblk):
    cols = []
    for b in range(nblk):
        at = place_ref[b] * blk + lax.broadcasted_iota(jnp.int32, (blk, DH), 0)
        cols.append(jnp.where(2 * at < limit, 0.0, NEG))
    return jnp.concatenate(cols, axis=0)


def dot_tn(a, b):
    return lax.dot_general(a, b, (((0,), (0,)), ((), ())), preferred_element_type=F32)


def in_vmem(args):
    return [pl.BlockSpec(memory_space=pltpu.VMEM) for _ in args]


def scalars():
    return pl.BlockSpec(memory_space=pltpu.SMEM)


def attend_kernel(heads, nblk, place_ref, len_ref, *refs):
    xs, (w_ref, strip_ref), refs = refs[:nblk], refs[nblk : nblk + 2], refs[nblk + 2 :]
    outs, (qkv_ref, log_ref, att_ref, kaug_ref, qaug_ref, vt_ref) = refs[:nblk], refs[nblk:]
    blk = xs[0].shape[0]
    for b in range(nblk):
        qkv_ref[b * blk : (b + 1) * blk, :] = dot_nn(xs[b][...], w_ref[...]).astype(BF16)
    ok_col = mask_column(place_ref, len_ref[0], blk, nblk)
    width = heads * DH
    for head in range(heads):
        at = head * DH
        qaug_ref[...] = query_side(qkv_ref[:, at : at + DH])
        kaug_ref[...] = key_side(qkv_ref[:, width + at : width + at + DH], ok_col)
        vt_ref[...] = qkv_ref[:, 2 * width + at : 2 * width + at + DH].T

        def one_block(qb, carry):
            q_at = pl.multiple_of(qb * blk, blk)
            query = qaug_ref[pl.ds(q_at, blk), :]
            parts = []
            for kb in range(nblk):
                m_at = pl.multiple_of(tile_at(place_ref, kb, qb, nblk) * blk, blk)
                parts.append(dot_nt(kaug_ref[kb * blk : (kb + 1) * blk, :], query) + strip_ref[head, pl.ds(m_at, blk), :])
            top = functools.reduce(jnp.maximum, [jnp.max(p, axis=0, keepdims=True) for p in parts])
            total = jnp.zeros((1, blk), F32)
            acc = jnp.zeros((DH, blk), F32)
            for kb in range(nblk):
                weight = jnp.exp(parts[kb] - top)
                total += jnp.sum(weight, axis=0, keepdims=True)
                acc += dot_nn(vt_ref[:, kb * blk : (kb + 1) * blk], weight.astype(BF16))
            att_ref[pl.ds(q_at, blk), at : at + DH] = (acc / total).T.astype(BF16)
            log_ref[head, pl.ds(qb, 1), :] = top + jnp.log(total)
            return carry

        lax.fori_loop(0, nblk, one_block, 0)
    for b in range(nblk):
        outs[b][...] = att_ref[b * blk : (b + 1) * blk, :]


def attend(place, row_len, xs, w_qkv, strips):
    nblk = len(xs)
    blk = xs[0].shape[0]
    heads = strips.shape[0]
    tokens = nblk * blk
    outs = [jax.ShapeDtypeStruct((blk, heads * DH), BF16)] * nblk + [
        jax.ShapeDtypeStruct((tokens, 3 * heads * DH), BF16),
        jax.ShapeDtypeStruct((heads, nblk, blk), F32),
    ]
    args = [*xs, w_qkv, strips]
    got = pl.pallas_call(
        functools.partial(attend_kernel, heads, nblk),
        in_specs=[scalars(), scalars(), *in_vmem(args)],
        out_specs=in_vmem(outs),
        out_shape=outs,
        scratch_shapes=[
            pltpu.VMEM((tokens, heads * DH), BF16),
            pltpu.VMEM((tokens, 2 * DH), BF16),
            pltpu.VMEM((tokens, 2 * DH), BF16),
            pltpu.VMEM((DH, tokens), BF16),
        ],
        compiler_params=pltpu.CompilerParams(vmem_limit_bytes=48 << 20),
        cost_estimate=pl.CostEstimate(flops=48 * heads * tokens * tokens * DH, bytes_accessed=8 << 20, transcendentals=heads * tokens * tokens),
        name="attend",
    )(place, row_len, *args)
    return got[:nblk], got[nblk], got[nblk + 1]


def attend_back_kernel(heads, nblk, first, final, place_ref, len_ref, *refs):
    xs, (w_ref, qkv_ref), refs = refs[:nblk], refs[nblk : nblk + 2], refs[nblk + 2 :]
    os, dos, (log_ref, strip_ref), refs = refs[:nblk], refs[nblk : 2 * nblk], refs[2 * nblk : 2 * nblk + 2], refs[2 * nblk + 2 :]
    sum_in = None
    if not first:
        sum_in, refs = refs[0], refs[1:]
    dns, (sum_ref, drev_ref), refs = refs[:nblk], refs[nblk : nblk + 2], refs[nblk + 2 :]
    grads_ref, kaug_ref, qaug_ref, kt_ref, dk_ref, dv_ref, o_ref, do_ref, dqkv_ref = refs
    blk = xs[0].shape[0]
    for b in range(nblk):
        o_ref[b * blk : (b + 1) * blk, :] = os[b][...]
        do_ref[b * blk : (b + 1) * blk, :] = dos[b][...]
    ok_col = mask_column(place_ref, len_ref[0], blk, nblk)
    width = heads * DH
    for head in range(heads):
        grads_ref[head] = jnp.zeros(grads_ref.shape[1:], F32)
        at = head * DH
        qaug_ref[...] = query_side(qkv_ref[:, at : at + DH])
        key = qkv_ref[:, width + at : width + at + DH]
        kaug_ref[...] = key_side(key, ok_col)
        kt_ref[...] = key.T
        dk_ref[...] = jnp.zeros_like(dk_ref)
        dv_ref[...] = jnp.zeros_like(dv_ref)

        def one_block(qb, carry):
            q_at = pl.multiple_of(qb * blk, blk)
            query = qaug_ref[pl.ds(q_at, blk), :]
            dout = do_ref[pl.ds(q_at, blk), at : at + DH]
            prod = dout.astype(F32) * o_ref[pl.ds(q_at, blk), at : at + DH].astype(F32)
            inner = jnp.sum(prod.T, axis=0, keepdims=True)
            log_row = log_ref[head, pl.ds(qb, 1), :]
            dqt = jnp.zeros((DH, blk), F32)
            for kb in range(nblk):
                here = slice(kb * blk, (kb + 1) * blk)
                m_at = pl.multiple_of(tile_at(place_ref, kb, qb, nblk) * blk, blk)
                score = dot_nt(kaug_ref[here, :], query) + strip_ref[head, pl.ds(m_at, blk), :]
                prob = jnp.exp(score - log_row)
                d_prob = dot_nt(qkv_ref[here, 2 * width + at : 2 * width + at + DH], dout)
                d_score = prob * (d_prob - inner)
                low = d_score.astype(BF16)
                grads_ref[head, pl.ds(m_at, blk), :] += d_score
                dv_ref[here, :] += dot_nn(prob.astype(BF16), dout)
                dk_ref[here, :] += dot_nn(low, query[:, :DH])
                dqt += dot_nn(kt_ref[:, here], low)
            dqkv_ref[pl.ds(q_at, blk), at : at + DH] = dqt.T.astype(BF16)
            return carry

        lax.fori_loop(0, nblk, one_block, 0)
        dqkv_ref[:, width + at : width + at + DH] = dk_ref[...].astype(BF16)
        dqkv_ref[:, 2 * width + at : 2 * width + at + DH] = dv_ref[...].astype(BF16)

    total = None
    for b in range(nblk):
        here = dqkv_ref[b * blk : (b + 1) * blk, :]
        dns[b][...] = dot_nt(here, w_ref[...]).astype(BF16)
        grad = dot_tn(xs[b][...], here)
        total = grad if total is None else total + grad
    if not first:
        total += sum_in[...]
    sum_ref[...] = total.astype(BF16).reshape(sum_ref.shape) if final else total

    flip = (
        lax.broadcasted_iota(jnp.int32, (blk, blk), 0) + lax.broadcasted_iota(jnp.int32, (blk, blk), 1) == blk - 1
    ).astype(F32).astype(BF16)
    drev_ref[...] = jnp.zeros_like(drev_ref)
    for head in range(heads):
        for part in range(5):
            low = (nblk + 1 - part) * blk
            grad = grads_ref[head, part * blk : (part + 1) * blk, :]
            if part in (0, 4):
                whole = jnp.sum(jnp.sum(grad, axis=0, keepdims=True), axis=1, keepdims=True)
                drev_ref[head : head + 1, low + blk : low + blk + 1] += whole
                continue
            high = grad.astype(BF16)
            rest = (grad - high.astype(F32)).astype(BF16)
            turned = dot_nn(flip, high) + dot_nn(flip, rest)
            wide = jnp.concatenate([jnp.zeros((blk, blk), F32), turned], axis=1)
            moved = pltpu.roll(wide, blk + 1, 1, stride=1, stride_axis=0)
            drev_ref[head : head + 1, low : low + 2 * blk] += jnp.sum(moved, axis=0, keepdims=True)


def attend_back(place, row_len, xs, w_qkv, qkv, outs, douts, logs, strips, sum_in, parts):
    nblk = len(xs)
    blk, d_model = xs[0].shape
    heads = strips.shape[0]
    tokens = nblk * blk
    cols = 3 * heads * DH
    args = [*xs, w_qkv, qkv, *outs, *douts, logs, strips] + ([] if sum_in is None else [sum_in])
    sum_shape = jax.ShapeDtypeStruct((parts, d_model // parts, cols), BF16) if parts else jax.ShapeDtypeStruct((d_model, cols), F32)
    shapes = [jax.ShapeDtypeStruct((blk, d_model), BF16)] * nblk + [sum_shape, jax.ShapeDtypeStruct((heads, 2 * tokens), F32)]
    got = pl.pallas_call(
        functools.partial(attend_back_kernel, heads, nblk, sum_in is None, bool(parts)),
        in_specs=[scalars(), scalars(), *in_vmem(args)],
        out_specs=in_vmem(shapes),
        out_shape=shapes,
        scratch_shapes=[
            pltpu.VMEM((heads, 5 * blk, blk), F32),
            pltpu.VMEM((tokens, 2 * DH), BF16),
            pltpu.VMEM((tokens, 2 * DH), BF16),
            pltpu.VMEM((DH, tokens), BF16),
            pltpu.VMEM((tokens, DH), F32),
            pltpu.VMEM((tokens, DH), F32),
            pltpu.VMEM((tokens, heads * DH), BF16),
            pltpu.VMEM((tokens, heads * DH), BF16),
            pltpu.VMEM((tokens, cols), BF16),
        ],
        compiler_params=pltpu.CompilerParams(vmem_limit_bytes=56 << 20),
        cost_estimate=pl.CostEstimate(flops=120 * heads * tokens * tokens * DH, bytes_accessed=16 << 20, transcendentals=heads * tokens * tokens),
        name="attend_back",
    )(place, row_len, *args)
    return got[:nblk], got[nblk], got[nblk + 1]


EPS = 1e-06


def project_kernel(nblk, rows, place_ref, *refs):
    cols_refs, refs = refs[:nblk], refs[nblk:]
    atts, refs = refs[: rows * nblk], refs[rows * nblk :]
    hids, gain_ref, w_ref, outs = refs[:rows], refs[rows], refs[rows + 1], refs[rows + 2 :]
    cols = cols_refs[0].shape[1]
    for b in range(nblk):
        for g in range(nblk):

            @pl.when(place_ref[b] == g)
            def _():
                w_ref[:, g * cols : (g + 1) * cols] = cols_refs[b][...]

    for r in range(rows):
        hid = hids[r][...]
        for b in range(nblk):
            here = pl.ds(pl.multiple_of(place_ref[b] * cols, 16), cols)
            hid += dot_nn(atts[r * nblk + b][...], w_ref[here, :])
        outs[2 * r][...] = hid
        factor = lax.rsqrt(jnp.mean(hid * hid, axis=-1, keepdims=True) + EPS)
        outs[2 * r + 1][...] = (hid * factor * gain_ref[...]).astype(BF16)


def project(place, w_blocks, atts, hids, gain):
    rows, nblk = len(atts), len(w_blocks)
    width = w_blocks[0].shape[0]
    args = [*w_blocks, *[block for row in atts for block in row], *hids, gain]
    outs = [jax.ShapeDtypeStruct((width, hids[0].shape[1]), BF16)]
    for hid in hids:
        outs += [jax.ShapeDtypeStruct(hid.shape, F32), jax.ShapeDtypeStruct(hid.shape, BF16)]
    got = pl.pallas_call(
        functools.partial(project_kernel, nblk, rows),
        in_specs=[scalars(), *in_vmem(args)],
        out_specs=in_vmem(outs),
        out_shape=outs,
        compiler_params=pltpu.CompilerParams(vmem_limit_bytes=32 << 20),
        cost_estimate=pl.CostEstimate(flops=4 * rows * hids[0].shape[0] * width * width, bytes_accessed=3 << 20, transcendentals=0),
        name="project",
    )(place, *args)
    return got[0], got[1::2], got[2::2]


def norm_back(hid, gain, d_norm):
    factor = lax.rsqrt(jnp.mean(hid * hid, axis=-1, keepdims=True) + EPS)
    scaled = hid * factor
    weighted = d_norm * gain
    inner = jnp.mean(scaled * weighted, axis=-1, keepdims=True)
    return factor * (weighted - scaled * inner), jnp.sum(d_norm * scaled, axis=0, keepdims=True)


def project_back_kernel(nblk, pieces, row, first, final, place_ref, *refs):
    adds, atts, refs = refs[:pieces], refs[pieces : pieces + nblk], refs[pieces + nblk :]
    (w_ref, hid_ref, cot_ref, gain_ref), refs = refs[:4], refs[4:]
    sum_in = None
    if not first:
        sum_in, refs = refs[0], refs[1:]
    dhid_ref, gain_out, datts, sum_ref, acc_ref = refs[0], refs[1], refs[2 : 2 + nblk], refs[2 + nblk], refs[3 + nblk]
    d_norm = adds[0][...].astype(F32)
    for add in adds[1:]:
        d_norm += add[...].astype(F32)
    back, gain_grad = norm_back(hid_ref[...], gain_ref[...], d_norm)
    gain_out[...] = gain_grad
    d_hid = cot_ref[row].astype(F32) + back
    dhid_ref[...] = d_hid
    branch = d_hid.astype(BF16)
    cols = atts[0].shape[1]
    for b in range(nblk):
        here = pl.ds(pl.multiple_of(place_ref[b] * cols, 16), cols)
        datts[b][...] = dot_nt(branch, w_ref[here, :]).astype(BF16)
        grad = dot_tn(atts[b][...], branch)
        acc_ref[here, :] = grad if first else sum_in[here, :] + grad
    if final:
        sum_ref[...] = acc_ref[...].astype(BF16).reshape(sum_ref.shape)
    else:
        sum_ref[...] = acc_ref[...]


def project_back(place, adds, atts, w_out, hid, cot, row, gain, sum_in, parts):
    nblk = len(atts)
    blk, cols = atts[0].shape
    width, d_model = w_out.shape
    args = [*adds, *atts, w_out, hid, cot, gain] + ([] if sum_in is None else [sum_in])
    sum_shape = jax.ShapeDtypeStruct((parts, width // parts, d_model), BF16) if parts else jax.ShapeDtypeStruct((width, d_model), F32)
    outs = [jax.ShapeDtypeStruct(hid.shape, F32), jax.ShapeDtypeStruct((1, d_model), F32)]
    outs += [jax.ShapeDtypeStruct((blk, cols), BF16)] * nblk + [sum_shape]
    got = pl.pallas_call(
        functools.partial(project_back_kernel, nblk, len(adds), row, sum_in is None, bool(parts)),
        in_specs=[scalars(), *in_vmem(args)],
        out_specs=in_vmem(outs),
        out_shape=outs,
        scratch_shapes=[pltpu.VMEM((width, d_model), F32)],
        compiler_params=pltpu.CompilerParams(vmem_limit_bytes=32 << 20),
        cost_estimate=pl.CostEstimate(flops=8 * blk * width * d_model, bytes_accessed=6 << 20, transcendentals=0),
        name="project_back",
    )(place, *args)
    return got[0], got[1], got[2 : 2 + nblk], got[2 + nblk]


def first_back_kernel(pieces, *refs):
    adds, (hid_ref, dhid_ref, gain_ref, out_ref, low_ref, high_ref, gain_out) = refs[:pieces], refs[pieces:]
    d_norm = adds[0][...].astype(F32)
    for add in adds[1:]:
        d_norm += add[...].astype(F32)
    back, gain_grad = norm_back(hid_ref[...], gain_ref[...], d_norm)
    gain_out[...] = gain_grad
    d_hid = dhid_ref[...] + back
    out_ref[...] = d_hid
    low_ref[...] = d_hid[:8]
    high_ref[...] = d_hid[-8:]


def first_back(adds, hid, d_hid, gain):
    args = [*adds, hid, d_hid, gain]
    d_model = hid.shape[1]
    outs = [jax.ShapeDtypeStruct(s, F32) for s in (hid.shape, (8, d_model), (8, d_model), (1, d_model))]
    return pl.pallas_call(
        functools.partial(first_back_kernel, len(adds)),
        in_specs=in_vmem(args),
        out_specs=in_vmem(outs),
        out_shape=outs,
        compiler_params=pltpu.CompilerParams(vmem_limit_bytes=32 << 20),
        cost_estimate=pl.CostEstimate(flops=20 * hid.shape[0] * d_model, bytes_accessed=4 << 20, transcendentals=0),
        name="first_back",
    )(*args)


EDGE = 8


def split_two(x):
    high = x.astype(BF16)
    return high, (x - high.astype(F32)).astype(BF16)


def dot_fine(dot, a, b):
    a_high, a_rest = split_two(a)
    b_high, b_rest = split_two(b)
    return dot(a_high, b_high) + (dot(a_high, b_rest) + dot(a_rest, b_high))


def dot_half(dot, a, b_low):
    a_high, a_rest = split_two(a)
    return dot(a_high, b_low) + dot(a_rest, b_low)


def same_block(first, frame, size):
    def group(axis, shape):
        place = lax.broadcasted_iota(jnp.int32, shape, axis) + first
        return jnp.floor((place.astype(F32) + 0.5) * (1.0 / size))

    return (group(0, (frame, 1)) == group(1, (1, frame))).astype(F32)


def unpack_front(pack_ref, wall_ref):
    parts, _, share = pack_ref.shape
    for d in range(parts):
        wall_ref[:, d * share : (d + 1) * share] = pack_ref[d]


def front_kernel(vocab, at_ref, len_ref, ids_ref, pack_ref, hid_ref, norm_ref, conv_ref, mask_ref, share_ref, wall_ref, tri_ref, quad_ref, pair_ref, x_ref):
    row = pl.program_id(0)
    frame = ids_ref.shape[2]
    tok = hid_ref.shape[1]
    first = at_ref[0] - EDGE

    @pl.when(row == 0)
    def _():
        unpack_front(pack_ref, wall_ref)
        for ref, size in ((pair_ref, 2), (tri_ref, 3), (quad_ref, 4)):
            ref[...] = same_block(first + 12 * EDGE, frame, size).astype(BF16)

    limit = len_ref[row]
    pad = wall_ref.shape[0]
    place_row = lax.broadcasted_iota(jnp.int32, (1, frame), 1) + first
    live_row = (place_row >= 0) & (place_row < limit)
    ids = jnp.where(live_row, ids_ref[0], -1)
    onehot = (lax.broadcasted_iota(jnp.int32, (pad, frame), 0) == ids).astype(F32).astype(BF16)
    masked = lax.dot_general(onehot, wall_ref[...], (((0,), (0,)), ((), ())), preferred_element_type=F32)
    mask_ref[0] = masked[EDGE : frame - EDGE].astype(BF16)
    x_ref[0:EDGE, :] = jnp.zeros((EDGE, masked.shape[1]), F32)
    x_ref[EDGE : EDGE + frame, :] = masked
    x_ref[EDGE + frame :, :] = jnp.zeros((EDGE, masked.shape[1]), F32)
    vectors = wall_ref[pad - 16 :, :].astype(F32)
    base = vocab - (pad - 16)
    place_col = lax.broadcasted_iota(jnp.int32, (frame, 1), 0) + first
    live_col = ((place_col >= 0) & (place_col < limit)).astype(F32)
    conv = vectors[base : base + 1] * x_ref[EDGE - 2 : EDGE - 2 + frame, :]
    for j in range(1, 4):
        conv += vectors[base + j : base + j + 1] * x_ref[EDGE - 2 + j : EDGE - 2 + j + frame, :]
    conv = conv * live_col
    conv_ref[0] = conv
    c_high, c_rest = split_two(conv)
    score_w = jnp.broadcast_to(vectors[base + 4 : base + 5], (8, conv.shape[1])).astype(BF16)
    single = (dot_nt(score_w, c_high) + dot_nt(score_w, c_rest))[0:1]
    s_high = single.astype(BF16).astype(F32)
    s_mid = (single - s_high).astype(BF16).astype(F32)
    stack = jnp.concatenate([s_high, s_mid, single - s_high - s_mid, jnp.zeros((5, frame), F32)], axis=0).astype(BF16)
    scores = [single]
    for ref, size in ((pair_ref, 2), (tri_ref, 3), (quad_ref, 4)):
        scores.append(jnp.sum(dot_nn(stack, ref[...]), axis=0, keepdims=True) * (1.0 / size))
    top = functools.reduce(jnp.maximum, scores)
    raw = [jnp.exp(s - top) for s in scores]
    total = raw[0] + raw[1] + raw[2] + raw[3]
    shares = jnp.concatenate([r / total for r in raw] + [jnp.zeros((4, frame), F32)], axis=0)
    share_ref[0] = shares
    cols = shares.T
    one = (lax.broadcasted_iota(jnp.int32, (frame, frame), 0) == lax.broadcasted_iota(jnp.int32, (frame, frame), 1))
    mix = jnp.where(one, cols[:, 0:1], 0.0)
    for at, (ref, size) in enumerate(((pair_ref, 2), (tri_ref, 3), (quad_ref, 4))):
        mix += ref[...].astype(F32) * (cols[:, at + 1 : at + 2] * (1.0 / size))
    start = 2 * lax.broadcasted_iota(jnp.int32, (tok, frame), 0) + EDGE
    here = lax.broadcasted_iota(jnp.int32, (tok, frame), 1)
    pool = jnp.where((here == start) | (here == start + 1), 0.5, 0.0).astype(BF16)
    m_high, m_rest = split_two(mix)
    weights = dot_nn(pool, m_high) + dot_nn(pool, m_rest)
    w_high, w_rest = split_two(weights)
    hid = dot_nn(w_high, c_high) + (dot_nn(w_high, c_rest) + dot_nn(w_rest, c_high))
    hid_ref[0] = hid
    factor = lax.rsqrt(jnp.mean(hid * hid, axis=-1, keepdims=True) + EPS)
    norm_ref[0] = (hid * factor * vectors[base + 5 : base + 6]).astype(BF16)


def front_forward(at, row_len, ids, pack, vocab, d_model):
    rows, _, frame = ids.shape
    extent = frame - 2 * EDGE
    tok = extent // 2
    pad = pack.shape[1]
    by_row = lambda r, *_: (r, 0, 0)
    return pl.pallas_call(
        functools.partial(front_kernel, vocab),
        grid_spec=pltpu.PrefetchScalarGridSpec(
            num_scalar_prefetch=2,
            grid=(rows,),
            in_specs=[
                pl.BlockSpec((1, 1, frame), by_row),
                pl.BlockSpec(pack.shape, lambda r, *_: (0, 0, 0)),
            ],
            out_specs=[
                pl.BlockSpec((1, tok, d_model), by_row),
                pl.BlockSpec((1, tok, d_model), by_row),
                pl.BlockSpec((1, frame, d_model), by_row),
                pl.BlockSpec((1, extent, d_model), by_row),
                pl.BlockSpec((1, 8, frame), by_row),
            ],
            scratch_shapes=[
                pltpu.VMEM((pad, d_model), BF16),
                pltpu.VMEM((frame, frame), BF16),
                pltpu.VMEM((frame, frame), BF16),
                pltpu.VMEM((frame, frame), BF16),
                pltpu.VMEM((frame + 2 * EDGE, d_model), F32),
            ],
        ),
        out_shape=[
            jax.ShapeDtypeStruct((rows, tok, d_model), F32),
            jax.ShapeDtypeStruct((rows, tok, d_model), BF16),
            jax.ShapeDtypeStruct((rows, frame, d_model), F32),
            jax.ShapeDtypeStruct((rows, extent, d_model), BF16),
            jax.ShapeDtypeStruct((rows, 8, frame), F32),
        ],
        compiler_params=pltpu.CompilerParams(vmem_limit_bytes=48 << 20),
        cost_estimate=pl.CostEstimate(flops=rows * 8 * frame * frame * d_model, bytes_accessed=rows * frame * d_model * 9, transcendentals=0),
        name="front",
    )(at, row_len, ids, pack)


def front_back_kernel(vocab, at_ref, len_ref, ids_ref, pack_ref, dhid_ref, rim_ref, conv_ref, mask_ref, share_ref, gain_ref, din_ref, grad_ref,
                      wall_ref, tri_ref, quad_ref, pair_ref, dconv_ref, sum_ref):
    row = pl.program_id(0)
    frame = ids_ref.shape[2]
    tok = dhid_ref.shape[1]
    extent = frame - 2 * EDGE
    first = at_ref[0] - EDGE
    pad = wall_ref.shape[0]

    @pl.when(row == 0)
    def _():
        unpack_front(pack_ref, wall_ref)
        for ref, size in ((pair_ref, 2), (tri_ref, 3), (quad_ref, 4)):
            ref[...] = same_block(first + 12 * EDGE, frame, size).astype(BF16)
        sum_ref[...] = jnp.zeros_like(sum_ref)

    limit = len_ref[row]
    vectors = wall_ref[pad - 16 :, :].astype(F32)
    base = vocab - (pad - 16)
    shares = [share_ref[0, b : b + 1, :] for b in range(4)]
    one = (lax.broadcasted_iota(jnp.int32, (frame, frame), 0) == lax.broadcasted_iota(jnp.int32, (frame, frame), 1)).astype(F32)
    masks = [one] + [ref[...].astype(F32) * (1.0 / size) for ref, size in ((pair_ref, 2), (tri_ref, 3), (quad_ref, 4))]
    mix = functools.reduce(jnp.add, [m * s for m, s in zip(masks, shares)])
    start = 2 * lax.broadcasted_iota(jnp.int32, (frame, tok), 1) + EDGE
    here = lax.broadcasted_iota(jnp.int32, (frame, tok), 0)
    pool = jnp.where((here == start) | (here == start + 1), 0.5, 0.0).astype(BF16)
    rim_at = lax.broadcasted_iota(jnp.int32, (frame, EDGE), 1)
    rim_start = 2 * rim_at + jnp.where(rim_at < EDGE // 2, 0, extent)
    rim_here = lax.broadcasted_iota(jnp.int32, (frame, EDGE), 0)
    rim_pool = jnp.where((rim_here == rim_start) | (rim_here == rim_start + 1), 0.5, 0.0).astype(BF16)
    m_high, m_rest = split_two(mix)
    conv = conv_ref[0]
    c_high, c_rest = split_two(conv)
    d_conv = jnp.zeros(conv.shape, F32)
    cross = jnp.zeros((frame, frame), F32)
    for ref, spread in ((dhid_ref, pool), (rim_ref, rim_pool)):
        d_high, d_rest = split_two(ref[0])
        weights = dot_nn(m_high, spread) + dot_nn(m_rest, spread)
        w_high, w_rest = split_two(weights)
        d_conv += dot_nn(w_high, d_high) + (dot_nn(w_high, d_rest) + dot_nn(w_rest, d_high))
        pairs = dot_nt(c_high, d_high) + (dot_nt(c_high, d_rest) + dot_nt(c_rest, d_high))
        cross += dot_half(dot_nt, pairs, spread)
    d_shares = [jnp.sum(m * cross, axis=0, keepdims=True) for m in masks]
    inner = functools.reduce(jnp.add, [s * d for s, d in zip(shares, d_shares)])
    d_single = jnp.sum(
        functools.reduce(jnp.add, [m * (s * (d - inner)) for m, s, d in zip(masks, shares, d_shares)]), axis=1, keepdims=True
    )
    own_col = lax.broadcasted_iota(jnp.int32, (frame, 1), 0)
    place_col = own_col + first
    live_col = ((place_col >= 0) & (place_col < limit)).astype(F32)
    own = ((own_col >= EDGE) & (own_col < frame - EDGE)).astype(F32)
    dconv_ref[...] = (d_conv + d_single * vectors[base + 4 : base + 5]) * live_col
    grad_score = jnp.sum(conv * (d_single * own), axis=0, keepdims=True)
    masked = mask_ref[0].astype(F32)
    d_masked = jnp.zeros(masked.shape, F32)
    for j in range(4):
        moved = dconv_ref[EDGE + 2 - j : EDGE + 2 - j + extent, :]
        d_masked += vectors[base + j : base + j + 1] * moved
        sum_ref[vocab + j : vocab + j + 1, :] += jnp.sum(masked * moved, axis=0, keepdims=True)
    sum_ref[vocab + 4 : vocab + 5, :] += grad_score
    d_in = (d_masked * live_col[EDGE : frame - EDGE]).astype(BF16)
    din_ref[0] = d_in
    ids = ids_ref[0][:, EDGE : frame - EDGE]
    emb_rows = -(-vocab // 8) * 8
    onehot = (lax.broadcasted_iota(jnp.int32, (emb_rows, extent), 0) == ids).astype(F32).astype(BF16)
    sum_ref[0:emb_rows, :] += dot_nn(onehot, d_in)

    @pl.when(row == pl.num_programs(0) - 1)
    def _():
        sum_ref[vocab + 5 : vocab + 7, :] = gain_ref[0:2, :]
        parts, _, share = grad_ref.shape
        for d in range(parts):
            grad_ref[d] = sum_ref[:, d * share : (d + 1) * share].astype(BF16)


def front_backward(at, row_len, ids, pack, d_hid, rims, conv, masked, shares, gains, vocab):
    rows, _, frame = ids.shape
    extent = frame - 2 * EDGE
    tok, d_model = d_hid.shape[1:]
    pad = pack.shape[1]
    by_row = lambda r, *_: (r, 0, 0)
    return pl.pallas_call(
        functools.partial(front_back_kernel, vocab),
        grid_spec=pltpu.PrefetchScalarGridSpec(
            num_scalar_prefetch=2,
            grid=(rows,),
            in_specs=[
                pl.BlockSpec((1, 1, frame), by_row),
                pl.BlockSpec(pack.shape, lambda r, *_: (0, 0, 0)),
                pl.BlockSpec((1, tok, d_model), by_row),
                pl.BlockSpec((1, EDGE, d_model), by_row),
                pl.BlockSpec((1, frame, d_model), by_row),
                pl.BlockSpec((1, extent, d_model), by_row),
                pl.BlockSpec((1, 8, frame), by_row),
                pl.BlockSpec(gains.shape, lambda r, *_: (0, 0)),
            ],
            out_specs=[
                pl.BlockSpec((1, extent, d_model), by_row),
                pl.BlockSpec(pack.shape, lambda r, *_: (0, 0, 0)),
            ],
            scratch_shapes=[
                pltpu.VMEM((pad, d_model), BF16),
                pltpu.VMEM((frame, frame), BF16),
                pltpu.VMEM((frame, frame), BF16),
                pltpu.VMEM((frame, frame), BF16),
                pltpu.VMEM((frame, d_model), F32),
                pltpu.VMEM((pad, d_model), F32),
            ],
        ),
        out_shape=[
            jax.ShapeDtypeStruct((rows, extent, d_model), BF16),
            jax.ShapeDtypeStruct(pack.shape, BF16),
        ],
        compiler_params=pltpu.CompilerParams(vmem_limit_bytes=56 << 20),
        cost_estimate=pl.CostEstimate(flops=rows * 16 * frame * frame * d_model, bytes_accessed=rows * frame * d_model * 12, transcendentals=0),
        name="front_back",
    )(at, row_len, ids, pack, d_hid, rims, conv, masked, shares, gains)


GELU_C = 0.7978845608
GELU_A = 0.044715


def pack_down(x):
    rows, third = x.shape[1], x.shape[2] // 3
    left, mid, right = x[..., :third], x[..., third : 2 * third], x[..., 2 * third :]
    return jnp.concatenate(
        [jnp.concatenate([left, right[:, : rows // 2]], axis=1), jnp.concatenate([mid, right[:, rows // 2 :]], axis=1)], axis=2
    )


def unpack_down(x):
    rows, third = x.shape[1] * 2 // 3, x.shape[2] // 2
    right = jnp.concatenate([x[:, rows:, :third], x[:, rows:, third:]], axis=1)
    return jnp.concatenate([x[:, :rows, :third], x[:, :rows, third:], right], axis=2)


def feed_kernel(nblk, rows, row, sizes, *refs):
    share, ff_cols, width, down_rows = sizes
    x_refs, cot_refs, rest_ref = refs[:nblk], refs[nblk : 2 * nblk], refs[2 * nblk]
    refs = refs[2 * nblk + 1 :]
    sums_in, outs_in = None, ()
    if row > 0:
        outs_in, sums_in, refs = refs[:nblk], refs[nblk : nblk + 2], refs[nblk + 2 :]
    outs, dnorms, grads = refs[:nblk], refs[nblk : 2 * nblk], refs[2 * nblk :]
    if row == rows - 1:
        pack_ref, sum_a, sum_b = grads
    else:
        sum_a, sum_b = grads
    parts = rest_ref.shape[0]
    w_in = rest_ref[:, :share, : 2 * ff_cols].reshape(parts * share, 2 * ff_cols)
    w_down = unpack_down(rest_ref[:, :, 2 * ff_cols :]).reshape(parts * down_rows, width)
    for b in range(nblk):
        x, cot = x_refs[b][...], cot_refs[b][row]
        both = dot_nn(x, w_in)
        gate, up = both[:, :ff_cols], both[:, ff_cols:]
        square = gate * gate
        turned = jnp.tanh(GELU_C * gate * (1.0 + GELU_A * square))
        half = 0.5 * (1.0 + turned)
        gelu = gate * half
        slope = half + (0.5 * GELU_C) * gate * (1.0 - turned * turned) * (1.0 + (3.0 * GELU_A) * square)
        hidden = (gelu * up).astype(BF16)
        if row > 0:
            outs[b][:row] = outs_in[b][...]
        outs[b][row] = dot_nn(hidden, w_down).astype(BF16)
        d_hidden = dot_nt(cot, w_down)
        d_both = jnp.concatenate([(d_hidden * up * slope).astype(BF16), (d_hidden * gelu).astype(BF16)], axis=1)
        dnorms[b][...] = dot_nt(d_both, w_in).astype(BF16)
        grad_a, grad_b = dot_tn(x, d_both), dot_tn(hidden, cot)
        if b == 0 and sums_in is None:
            sum_a[...] = grad_a
            sum_b[...] = grad_b
        elif b == 0:
            sum_a[...] = sums_in[0][...] + grad_a
            sum_b[...] = sums_in[1][...] + grad_b
        else:
            sum_a[...] += grad_a
            sum_b[...] += grad_b
    if row == rows - 1:
        pack_ref[:, :, : 2 * ff_cols] = sum_a[...].astype(BF16).reshape(parts, share, 2 * ff_cols)
        pack_ref[:, :, 2 * ff_cols :] = pack_down(sum_b[...].astype(BF16).reshape(parts, down_rows, width))


def feed(xs, cots, rest, before, row, sizes):
    nblk = len(xs)
    tok, d_model = xs[0].shape
    share, ff_cols, width, down_rows = sizes
    parts, rows = rest.shape[0], cots[0].shape[0]
    sum_shapes = [(d_model, 2 * ff_cols), (parts * down_rows, width)]
    outs = [jax.ShapeDtypeStruct((row + 1, tok, width), BF16)] * nblk + [jax.ShapeDtypeStruct((tok, d_model), BF16)] * nblk
    scratch = []
    if row == rows - 1:
        outs.append(jax.ShapeDtypeStruct(rest.shape, BF16))
        scratch = [pltpu.VMEM(s, F32) for s in sum_shapes]
    else:
        outs += [jax.ShapeDtypeStruct(s, F32) for s in sum_shapes]
    args = [*xs, *cots, rest, *before]
    flops = 2 * nblk * tok * d_model * ff_cols * 9
    got = pl.pallas_call(
        functools.partial(feed_kernel, nblk, rows, row, sizes),
        in_specs=in_vmem(args),
        out_specs=in_vmem(outs),
        out_shape=outs,
        scratch_shapes=scratch,
        compiler_params=pltpu.CompilerParams(vmem_limit_bytes=56 << 20),
        cost_estimate=pl.CostEstimate(flops=flops, bytes_accessed=12 << 20, transcendentals=nblk * tok * ff_cols),
        name="feed",
    )(*args)
    return got[:nblk], got[nblk : 2 * nblk], got[2 * nblk :]


P = jax.sharding.PartitionSpec


def rims_of(x, width):
    size, length = lax.axis_size("seq"), x.shape[1]
    up = [(i, i + 1) for i in range(size - 1)]
    down = [(j, i) for i, j in up]
    before = lax.ppermute(x[:, length - width :], "seq", up)
    after = lax.ppermute(x[:, :width], "seq", down)
    return before, after


def flip_with(x, axis, bit):
    return lax.ppermute(x, axis, [(i, i ^ bit) for i in range(lax.axis_size(axis))])


def bits_of(axis):
    bits, bit = [], 1
    while bit < lax.axis_size(axis):
        bits.append(bit)
        bit *= 2
    return bits[::-1]


def after(x, *others):
    return lax.optimization_barrier((x,) + others)[0]


def places_of(n):
    places = [0]
    bit = n // 2
    while bit:
        places = places + [p ^ bit for p in places]
        bit //= 2
    return places


def swap_blocks(parts):
    return [part if bit == 0 else flip_with(part, "seq", bit) for part, bit in zip(parts, places_of(len(parts)))]


def gather_direct(x):
    return swap_blocks([x] * lax.axis_size("seq"))


def gather_first(x):
    blocks = [x]
    for bit in bits_of("seq")[:-1]:
        blocks = blocks + [flip_with(block, "seq", bit) for block in blocks]
    return blocks


def gather_last(blocks):
    return blocks + [flip_with(block, "seq", 1) for block in blocks]


def gather_two(x):
    return gather_last(gather_first(x))


def scatter_first(parts):
    half = len(parts) // 2
    got = [flip_with(part, "seq", 1) for part in parts[half:]]
    send = [(a.astype(F32) + b.astype(F32)).astype(BF16) for a, b in zip(parts[1:half], got[1:])]
    return [parts[0], got[0]], send


def scatter_last(own, send):
    return own + [flip_with(part, "seq", place) for part, place in zip(send, places_of(2 * len(send) + 2)[1:])]


def add_up(parts):
    return functools.reduce(jnp.add, [part.astype(F32) for part in parts])


def swap_dp(x):
    return lax.all_to_all(x, "dp", split_axis=0, concat_axis=0, tiled=True)


def sum_parts(x):
    return jnp.sum(x.astype(F32), axis=0)


def gather_step(x, bit):
    axis = bits_of("dp").index(bit)
    other = flip_with(x, "dp", bit)
    upper = (lax.axis_index("dp") & bit) != 0
    return jnp.concatenate([jnp.where(upper, other, x), jnp.where(upper, x, other)], axis=axis)


def gather_start(x):
    return x.reshape((1,) * len(bits_of("dp")) + x.shape)


def sum_seq(x):
    for bit in bits_of("seq")[::-1]:
        x = x + flip_with(x.astype(BF16), "seq", bit).astype(F32)
    return x


def in_order(blocks, me):
    n = len(blocks)
    bits = bits_of("seq")
    x = jnp.stack(blocks).reshape((2,) * len(bits) + blocks[0].shape)
    for at, bit in enumerate(bits[::-1]):
        upper = (me & bit) != 0
        x = jnp.where(upper, jnp.flip(x, at), x)
    x = x.transpose(tuple(range(len(bits)))[::-1] + tuple(range(len(bits), x.ndim)))
    return x.reshape((n,) + blocks[0].shape)


def on_device(
    byte_ids,
    lengths,
    deal_order,
    buckets,
    embedding,
    conv_w,
    score_w,
    gain_one,
    w_query,
    w_key,
    w_value,
    w_out,
    rel_bias,
    gain_two,
    w_gate,
    w_up,
    w_down,
    cotangent,
):
    n = lax.axis_size("seq")
    dp = lax.axis_size("dp")
    me = lax.axis_index("seq")
    rows_dev, extent = byte_ids.shape
    share, width = w_query.shape
    d_model = share * dp
    head_cols = width // n
    heads_dev = head_cols // DH
    ff_cols = w_gate.shape[1] // n
    down_rows = w_down.shape[0] // n
    tok = cotangent.shape[1]
    place = jnp.array(places_of(n), jnp.int32) ^ me

    vocab = embedding.shape[0]
    pad_vocab = -(-(vocab + 7) // 16) * 16
    front_pack = jnp.concatenate(
        [embedding, conv_w, score_w[None], gain_one[None], gain_two[None], jnp.zeros((pad_vocab - vocab - 7, share), BF16)], axis=0
    )

    def own_cols(weight):
        return lax.dynamic_slice_in_dim(weight, me * head_cols, head_cols, 1)

    qkv_pack = jnp.concatenate([own_cols(w_query), own_cols(w_key), own_cols(w_value), own_cols(w_out)], axis=1)
    front_all, qkv_w = gather_start(front_pack), gather_start(qkv_pack)
    up_bits = bits_of("dp")
    qkv_bits = up_bits[-1:] + up_bits[:-1]
    for at, bit in enumerate(up_bits):
        front_all = gather_step(front_all, bit)
        if at < len(up_bits) - 1:
            qkv_w = after(gather_step(qkv_w, qkv_bits[at]), front_all)
    front_all = front_all.reshape((dp,) + front_pack.shape)
    gain_first = front_all[:, vocab + 5].reshape(1, d_model).astype(F32)
    gain_second = front_all[:, vocab + 6].reshape(1, d_model).astype(F32)

    def own_ff(weight):
        return lax.dynamic_index_in_dim(weight.reshape(share, dp, n, down_rows), me, 2, keepdims=False).reshape(
            share, ff_cols
        )

    down_own = lax.dynamic_slice_in_dim(w_down, me * down_rows, down_rows, 0)
    rest_pack = jnp.concatenate([own_ff(w_gate), own_ff(w_up), pack_down(down_own[None])[0]], axis=1)
    rest_all = lax.all_gather(after(rest_pack, front_all), "dp", axis=0, tiled=False)

    offset = me * extent
    matches = deal_order[:, None] == jnp.arange(lengths.shape[0], dtype=jnp.int32)[None, :]
    row_len = jnp.sum(jnp.where(matches, lengths[None, :], 0), axis=1)
    rim_low, rim_high = rims_of(byte_ids, EDGE)
    ids = jnp.concatenate([rim_low, byte_ids, rim_high], axis=1)[:, None, :]
    at = jnp.full((1,), offset, jnp.int32)
    row_ids = range(rows_dev)
    lens = [row_len[r : r + 1] for r in row_ids]

    first_head = me * heads_dev
    bias_loc = lax.dynamic_slice_in_dim(rel_bias, first_head, heads_dev, 1)
    offsets = jnp.concatenate([jnp.full((1,), -1, jnp.int32), buckets[::-1]])
    onehot = (offsets[None, :] == jnp.arange(rel_bias.shape[0], dtype=jnp.int32)[:, None]).astype(BF16)
    strips = bias_strips(jnp.einsum("nh,nx->hx", bias_loc, onehot, preferred_element_type=F32), n)

    cots = gather_two(cotangent)
    normed, h_zero, kept = [], [], []
    gate = (strips,)
    for r in row_ids:
        h, low, *rest = front_forward(at, lens[r], after(ids[r : r + 1], *gate), front_all, vocab, d_model)
        if r == 0:
            qkv_w = gather_step(after(qkv_w, low), qkv_bits[-1])
        gate = (low,)
        h_zero.append(h[0])
        normed.append(low[0])
        kept.append(rest)
    low_one = [gather_two(low) if r == 0 else gather_direct(low) for r, low in enumerate(normed)]
    qkv_w = qkv_w.reshape(d_model, 4 * head_cols)
    out_blocks = gather_first(qkv_w[:, 3 * head_cols :])
    qkv_w = qkv_w[:, : 3 * head_cols]
    gate = gate + tuple(cots)
    atts, qkvs, logs, mixed = [], [], [], []
    for r in row_ids:
        xs = [after(low_one[r][0], *gate)] + list(low_one[r][1:])
        att, qkv, log = attend(place, lens[r], xs, qkv_w, strips)
        gate = (qkv,)
        atts.append(att)
        qkvs.append(qkv)
        logs.append(log)
        mixed.append(swap_blocks(att))
        if r == 0:
            out_blocks = gather_last([after(block, *gate) for block in out_blocks])
    w_out_all, h_one, lows = project(place, out_blocks, [[after(m[0], *gate)] + m[1:] for m in mixed], h_zero, gain_second)
    low_two = [gather_two(low) if r == 0 else gather_direct(low) for r, low in enumerate(lows)]
    sizes = (share, ff_cols, width, down_rows)
    d_norm_two, before = [], ()
    for r in row_ids:
        xs = [after(low_two[r][0], *gate)] + low_two[r][1:]
        ff_outs, d_norm, sums = feed(xs, cots, rest_all, before, r, sizes)
        before = (*ff_outs, *sums)
        gate = (d_norm[0],)
        d_norm_two.append(swap_blocks(d_norm) if r < rows_dev - 1 else scatter_last(*scatter_first(d_norm)))
    ff_sum = lax.psum_scatter(sums[0], "dp", scatter_dimension=0, tiled=False)
    d_h_one, gains_two, d_mixed, out_grad = [], [], [], None
    for r in row_ids:
        adds = [after(d_norm_two[r][0], *gate)] + d_norm_two[r][1:]
        d_h, gain_grad, d_att, out_grad = project_back(
            place, adds, mixed[r], w_out_all, h_one[r], cotangent, r, gain_second, out_grad, dp if r == rows_dev - 1 else 0
        )
        gate = (d_h,)
        d_h_one.append(d_h)
        gains_two.append(gain_grad)
        d_mixed.append(swap_blocks(d_att))
    ff_own, ff_send = scatter_first([after(ff_out, *gate) for ff_out in ff_outs])
    out_parts = swap_dp(out_grad)
    d_norms, qkv_grad, d_revs = [], None, []
    for r in row_ids:
        douts = [after(d_mixed[r][0], *gate)] + d_mixed[r][1:]
        d_norm, qkv_grad, d_rev = attend_back(
            place, lens[r], low_one[r], qkv_w, qkvs[r], atts[r], douts, logs[r], strips, qkv_grad, dp if r == rows_dev - 1 else 0
        )
        gate = (d_norm[0],)
        d_norms.append(d_norm)
        d_revs.append(d_rev)
        if r == 0:
            ff_send = [after(part, *gate) for part in ff_send]
            gate = gate + tuple(ff_send)
            ff_whole = scatter_last(ff_own, ff_send)
    output = (jnp.stack(h_one) + add_up([after(part, *gate) for part in ff_whole])).astype(BF16)
    qkv_parts = swap_dp(qkv_grad)
    d_rel_loc = jnp.einsum("nx,hx->nh", onehot.astype(F32), sum(d_revs), precision=lax.Precision.HIGHEST)
    d_rel = lax.dynamic_update_slice_in_dim(jnp.zeros(rel_bias.shape, F32), d_rel_loc, first_head, 1)
    rel_steps = [("seq", bit) for bit in bits_of("seq")[::-1]] + [("dp", bit) for bit in bits_of("dp")[::-1]]

    d_first = [swap_blocks(d_norm) for d_norm in d_norms[:-1]]
    last_own, last_send = scatter_first(d_norms[-1])
    d_first.append(scatter_last(last_own, last_send))
    g_out = sum_parts(out_parts)
    d_inputs, front_grads = [], []
    for r in row_ids:
        adds = [after(d_first[r][0], *gate)] + d_first[r][1:]
        d_h_zero, low_rim, high_rim, gain_grad = first_back(adds, h_zero[r], d_h_one[r], gain_first)
        size = lax.axis_size("seq")
        low_side = lax.ppermute(high_rim, "seq", [(i, i + 1) for i in range(size - 1)])[EDGE // 2 :]
        high_side = lax.ppermute(low_rim, "seq", [(i + 1, i) for i in range(size - 1)])[: EDGE // 2]
        rims = jnp.concatenate([low_side, high_side], axis=0)[None]
        d_rel = d_rel + flip_with(d_rel, *rel_steps.pop(0))
        if r == 0:
            rims = after(rims, d_rel, *last_send, g_out, ff_sum)
        conv_out, masked, shares = kept[r]
        d_in, front_grad = front_backward(
            at, lens[r], ids[r : r + 1], front_all, d_h_zero[None], rims, conv_out, masked, shares,
            jnp.concatenate([gain_grad, gains_two[r]], axis=0), vocab,
        )
        gate = (front_grad,)
        d_rel = after(d_rel, d_in)
        d_inputs.append(d_in[0])
        front_grads.append(front_grad)
    d_input = jnp.stack(d_inputs)
    front_parts = swap_dp(add_up(front_grads).astype(BF16))

    def every(x):
        return in_order(gather_two(x.astype(BF16)), me)

    ff_all = every(after(ff_sum, d_inputs[0]))
    g_gu = ff_all[:, :, : 2 * ff_cols].reshape(n, share, 2, dp, down_rows)
    g_gu = g_gu.transpose(2, 1, 3, 0, 4).reshape(2, share, n * ff_cols).astype(F32)
    g_down = unpack_down(ff_all[:, :, 2 * ff_cols :]).reshape(n * down_rows, width).astype(F32)
    while rel_steps:
        d_rel = d_rel + flip_with(d_rel, *rel_steps.pop(0))
    g_qkv = every(sum_parts(after(qkv_parts, *gate)).reshape(share, 3, head_cols))
    g_qkv = g_qkv.transpose(2, 1, 0, 3).reshape(3, share, width).astype(F32)
    g_out = sum_seq(after(g_out, *gate))
    front_sum = sum_seq(sum_parts(front_parts))
    return (
        output,
        d_input,
        front_sum[:vocab],
        front_sum[vocab : vocab + 4],
        front_sum[vocab + 4],
        front_sum[vocab + 5],
        g_qkv[0],
        g_qkv[1],
        g_qkv[2],
        g_out,
        d_rel,
        front_sum[vocab + 6],
        g_gu[0],
        g_gu[1],
        g_down,
    )


def solution(mesh):
    return jax.shard_map(
        on_device,
        mesh=mesh,
        in_specs=(
            P("dp", "seq"),
            P(),
            P("dp"),
            P(),
            P(None, "dp"),
            P(None, "dp"),
            P("dp"),
            P("dp"),
            P("dp", None),
            P("dp", None),
            P("dp", None),
            P("dp", None),
            P(),
            P("dp"),
            P("dp", None),
            P("dp", None),
            P("dp", None),
            P("dp", "seq", None),
        ),
        out_specs=(
            P("dp", "seq", None),
            P("dp", "seq", None),
            P(None, "dp"),
            P(None, "dp"),
            P("dp"),
            P("dp"),
            P("dp", None),
            P("dp", None),
            P("dp", None),
            P("dp", None),
            P(),
            P("dp"),
            P("dp", None),
            P("dp", None),
            P("dp", None),
        ),
        check_vma=False,
    )
```

time: 572 us -> 413 us (0.72)
  Pallas kernels: 64.1 us -> 165 us
  waiting for transfers between devices: 155 us -> 57.2 us
  other arithmetic: 110 us -> 26.2 us
  blocking collectives: 42.7 us -> 0 us
  matrix products: 43.1 us -> 1.8 us
  starting transfers between devices: 47.2 us -> 82.3 us
  local copies, waits for them, and re-layouts: 89.1 us -> 60.2 us
    pallas_call x2 -> x16, Pallas kernels: 64.1 us -> 165 us  [the longest x2 50.4 us: attend_back(): pl.pallas_call(functools.partial(attend_back_kernel, heads, nblk, sum_in...]
    ppermute x34 -> x66, waiting for transfers between devices: 139 us -> 55.3 us  [flip_with(): lax.ppermute(x, axis, [(i, i ^ bit) for i in range(lax.axis_size(axis))])]
    psum x1 -> x0, blocking collectives: 42.7 us -> none  [on_device(): grad_rel_bias = lax.psum(d_rel_full, ('dp', 'seq'))]
    dot_general x16 -> x2, matrix products: 43.1 us -> 1.8 us  [the longest x1 0.94 us: on_device(): jnp.einsum('nx,hx->nh', onehot.astype(F32), sum(d_revs), precision=lax.Pr...]
    reduce_sum x13 -> x3, other arithmetic: 38.4 us -> 3.98 us  [sum_parts(): return jnp.sum(x.astype(F32), axis=0)]
    mul x17 -> x0, other arithmetic: 25.4 us -> none  [the longest x10 22.5 us: block_means(): select[:, None] * padded[..., 3 + shift_at:3 + shift_at + extent, :]]
    ppermute x34 -> x66, starting transfers between devices: 32.5 us -> 55.5 us  [flip_with(): lax.ppermute(x, axis, [(i, i ^ bit) for i in range(lax.axis_size(axis))])]
    unnamed x179 -> x242, local copies, waits for them, and re-layouts: 19.7 us -> 39.5 us
  transfers between devices with their start and end apart: 43 -> 77, of which waited for: 17 -> 15; matrix products, arithmetic and copies ran while one was open for 30% -> 11% of each run, Pallas kernels for 4% -> 37%
where the time goes in v2:
time: 413 us; the launch traced here: 408 us
  Pallas kernels  165 us (40%)
  starting transfers between devices  82.3 us (20%)
  local copies, waits for them, and re-layouts  60.2 us (15%)
  waiting for transfers between devices  57.2 us (14%)
  other arithmetic  26.2 us (6%)
  between operations  15.7 us (4%)
    ppermute x66, starting transfers between devices, flip_with(): lax.ppermute(x, axis, [(i, i ^ bit) for i in range(lax.axis_size(axis))])  55.5 us
    ppermute x66, waiting for transfers between devices, flip_with(): lax.ppermute(x, axis, [(i, i ^ bit) for i in range(lax.axis_size(axis))])  55.3 us
    pallas_call x2, Pallas kernels, attend_back(): pl.pallas_call(functools.partial(attend_back_kernel, heads, nblk, sum_in...  50.4 us
    unnamed x242, local copies, waits for them, and re-layouts  39.5 us
    pallas_call x2, Pallas kernels, attend(): pl.pallas_call(functools.partial(attend_kernel, heads, nblk), in_specs=[s...  32.1 us
    pallas_call x2, Pallas kernels, feed(): pl.pallas_call(functools.partial(feed_kernel, nblk, rows, row, sizes), in...  29.1 us
    pallas_call x2, Pallas kernels, front_backward(): pl.pallas_call(functools.partial(front_back_kernel, vocab), grid_spec=plt...  26.5 us
    all_to_all x3, starting transfers between devices, swap_dp(): return lax.all_to_all(x, 'dp', split_axis=0, concat_axis=0, tiled=True)  15.8 us
  transfers between devices with their start and end apart: 77, of which 15 were waited for; matrix products, arithmetic and copies ran while one was open for 11% of the time, Pallas kernels for 37%

profile of v2, /device:TPU:0, one launch (start us, length us, event | category | flops | bytes accessed | tf_op | source)
XLA Modules:
  0.0 408.5 jit_solution(486134409700913711)
XLA Ops:
  9.6 4.1 collective-permute-start.1
  17.2 4.4 %collective-permute-start.8 = (bf16[2,256,768]{2,1,0:T(8,128)(2,1)}, bf16[2,256,768]{2,1,0:T(8,128)(2,1)}, u32[]{:S(2)}, u32[]{:S(2)}) collective-permute-start(bf16[2,256,768]{2,1,0:T(8,128)(2,1)} %refs_9_.1), channel_id=1, source_target_pairs={{0,2},{1,3},{2,0},{3,1},{4,6},{5,7},{6,4},{7,5},{8,10},{9,11},{10,... | collective-permute-start | bytes 2359304 | tf_op jit(solution)/shard_map/ppermute | solution.py:749
  37.7 5.4 %collective-permute-done.6 = bf16[2,2,1,272,96]{4,3,2,1,0:T(8,128)(2,1)S(1)} collective-permute-done((bf16[2,2,1,272,96]{4,3,2,1,0:T(8,128)(2,1)S(1)}, bf16[2,2,1,272,96]{4,3,2,1,0:T(8,128)(2,1)S(1)}, u32[]{:S(2)}, u32[]{:S(2)}) %collective-permute-start.6) | collective-permute-done | bytes 208928 | tf_op jit(solution)/shard_map/ppermute | solution.py:749
  44.5 6.5 %front.2 = (f32[1,256,768]{2,1,0:T(8,128)S(1)}, bf16[1,256,768]{2,1,0:T(8,128)(2,1)S(1)}, f32[1,528,768]{2,1,0:T(8,128)S(1)}, bf16[1,512,768]{2,1,0:T(8,128)(2,1)S(1)}, f32[1,8,528]{2,1,0:T(8,128)S(1)}) custom-call(s32[1]{0:T(128)} %bitcast.5.at_ref, s32[1]{0:T(128)} %get-tuple-element.357.len_ref, s32[1,1,528]{2,1,0:T(1,128)S(1)} %get-tuple-element.134.ids_ref, ...), custom_call_target="tpu_custom_call" | custom-call | flops 1712848896 | bytes 3649536 | tf_op jit(solution)/shard_map/front/pallas_call | solution.py:488
  57.0 6.5 %front.3 = (f32[1,256,768]{2,1,0:T(8,128)S(1)}, bf16[1,256,768]{2,1,0:T(8,128)(2,1)S(1)}, f32[1,528,768]{2,1,0:T(8,128)S(1)}, bf16[1,512,768]{2,1,0:T(8,128)(2,1)S(1)}, f32[1,8,528]{2,1,0:T(8,128)S(1)}) custom-call(s32[1]{0:T(128)} %bitcast.5.at_ref, s32[1]{0:T(128)} %get-tuple-element.356.len_ref, s32[1,1,528]{2,1,0:T(1,128)S(1)} %get-tuple-element.137.ids_ref, ...), custom_call_target="tpu_custom_call" | custom-call | flops 1712848896 | bytes 3649536 | tf_op jit(solution)/shard_map/front/pallas_call | solution.py:488
  66.3 9.0 %collective-permute-done.7 = bf16[2,1,2,96,768]{4,3,2,1,0:T(8,128)(2,1)S(1)} collective-permute-done((bf16[2,1,2,96,768]{4,3,2,1,0:T(8,128)(2,1)S(1)}, bf16[2,1,2,96,768]{4,3,2,1,0:T(8,128)(2,1)S(1)}, u32[]{:S(2)}, u32[]{:S(2)}) %collective-permute-start.7) | collective-permute-done | bytes 589856 | tf_op jit(solution)/shard_map/ppermute | solution.py:749
  78.2 16.5 %attend.2 = (bf16[256,192]{1,0:T(8,128)(2,1)S(1)}, bf16[256,192]{1,0:T(8,128)(2,1)S(1)}, bf16[256,192]{1,0:T(8,128)(2,1)}, bf16[256,192]{1,0:T(8,128)(2,1)}, bf1...) custom-call(s32[4]{0:T(128)S(1)} %broadcast_xor_fusion.place_ref, s32[1]{0:T(128)} %get-tuple-element.357.len_ref, ...), custom_call_target="tpu_custom_call" | custom-call | flops 9663676416 | bytes 8388608 | tf_op jit(solution)/shard_map/attend/pallas_call | solution.py:127
  97.6 15.6 %attend.3 = (bf16[256,192]{1,0:T(8,128)(2,1)S(1)}, bf16[256,192]{1,0:T(8,128)(2,1)S(1)}, bf16[256,192]{1,0:T(8,128)(2,1)S(1)}, bf16[256,192]{1,0:T(8,128)(2,1)S(...) custom-call(s32[4]{0:T(128)S(1)} %broadcast_xor_fusion.place_ref, s32[1]{0:T(128)} %get-tuple-element.356.len_ref, ...), custom_call_target="tpu_custom_call" | custom-call | flops 9663676416 | bytes 8388608 | tf_op jit(solution)/shard_map/attend/pallas_call | solution.py:127
  117.8 4.2 %collective-permute-done.23.refs_9_.refs_4_ = bf16[256,192]{1,0:T(8,128)(2,1)S(1)} collective-permute-done((bf16[256,192]{1,0:T(8,128)(2,1)S(1)}, bf16[256,192]{1,0:T(8,128)(2,1)S(1)}, u32[]{:S(2)}, u32[]{:S(2)}) %collective-permute-start.23) | collective-permute-done | bytes 98336 | tf_op jit(solution)/shard_map/ppermute | solution.py:749
  144.3 3.8 project.1
  149.4 10.3 %collective-permute-done.26.refs_1_ = bf16[256,768]{1,0:T(8,128)(2,1)S(1)} collective-permute-done((bf16[256,768]{1,0:T(8,128)(2,1)S(1)}, bf16[256,768]{1,0:T(8,128)(2,1)S(1)}, u32[]{:S(2)}, u32[]{:S(2)}) %collective-permute-start.26) | collective-permute-done | bytes 393248 | tf_op jit(solution)/shard_map/ppermute | solution.py:749
  162.6 13.4 %feed.2 = (bf16[1,256,768]{2,1,0:T(8,128)(2,1)}, bf16[1,256,768]{2,1,0:T(8,128)(2,1)}, bf16[1,256,768]{2,1,0:T(8,128)(2,1)}, bf16[1,256,768]{2,1,0:T(8,128)(2,1)...) custom-call(bf16[256,768]{1,0:T(8,128)(2,1)} %copy-done.65, ...), custom_call_target="tpu_custom_call" | custom-call | flops 7247757312 | bytes 12582912 | tf_op jit(solution)/shard_map/feed/pallas_call | solution.py:723
  176.0 3.5 collective-permute-done.31.refs_3_
  179.5 15.8 %feed.3 = (bf16[2,256,768]{2,1,0:T(8,128)(2,1)}, bf16[2,256,768]{2,1,0:T(8,128)(2,1)}, bf16[2,256,768]{2,1,0:T(8,128)(2,1)}, bf16[2,256,768]{2,1,0:T(8,128)(2,1)...) custom-call(bf16[256,768]{1,0:T(8,128)(2,1)} %get-tuple-element.164., ...), custom_call_target="tpu_custom_call" | custom-call | flops 7247757312 | bytes 12582912 | tf_op jit(solution)/shard_map/feed/pallas_call | solution.py:723
  200.2 7.6 %collective-permute-done.32.refs_1_ = bf16[256,768]{1,0:T(8,128)(2,1)} collective-permute-done((bf16[256,768]{1,0:T(8,128)(2,1)}, bf16[256,768]{1,0:T(8,128)(2,1)}, u32[]{:S(2)}, u32[]{:S(2)}) %collective-permute-start.32) | collective-permute-done | bytes 393248 | tf_op jit(solution)/shard_map/ppermute | solution.py:749
  207.8 7.2 %collective-permute-done.34.refs_3_ = bf16[256,768]{1,0:T(8,128)(2,1)} collective-permute-done((bf16[256,768]{1,0:T(8,128)(2,1)}, bf16[256,768]{1,0:T(8,128)(2,1)}, u32[]{:S(2)}, u32[]{:S(2)}) %collective-permute-start.34) | collective-permute-done | bytes 393248 | tf_op jit(solution)/shard_map/ppermute | solution.py:749
  226.1 3.7 project_back.3
  234.7 25.1 %attend_back.2 = (bf16[256,768]{1,0:T(8,128)(2,1)}, bf16[256,768]{1,0:T(8,128)(2,1)}, bf16[256,768]{1,0:T(8,128)(2,1)}, bf16[256,768]{1,0:T(8,128)(2,1)}, f32[768,576]{1,0:T(8,128)}, /*index=5*/f32[3,2048]{1,0:T(4,128)}) custom-call(s32[4]{0:T(128)} %copy-done.49, s32[1]{0:T(128)} %get-tuple-element.357.len_ref, bf16[256,768]{1,0:T(8,128)(2,1)} %bitcast.93, ...), custom_call_target="tpu_custom_call" | custom-call | flops 24159191040 | bytes 16777216 | tf_op jit(solution)/shard_map/attend_back/pallas_call | solution.py:235
  260.3 5.1 %all-to-all-start = ((bf16[8,96,768]{2,1,0:T(8,128)(2,1)}), bf16[8,96,768]{2,1,0:T(8,128)(2,1)}, u32[]{:S(2)}, u32[]{:S(2)}) async-start(bf16[8,96,768]{2,1,0:T(8,128)(2,1)} %get-tuple-element.222), calls=%async_computation | async-start | bytes 2359296 | tf_op jit(solution)/shard_map/all_to_all | solution.py:812
  269.0 25.4 %attend_back.3 = (bf16[256,768]{1,0:T(8,128)(2,1)}, bf16[256,768]{1,0:T(8,128)(2,1)}, bf16[256,768]{1,0:T(8,128)(2,1)}, bf16[256,768]{1,0:T(8,128)(2,1)}, bf16[8...) custom-call(s32[4]{0:T(128)} %copy-done.49, s32[1]{0:T(128)} %get-tuple-element.356.len_ref, bf16[256,768]{1,0:T(8,128)(2,1)} %bitcast.89, ...), custom_call_target="tpu_custom_call" | custom-call | flops 24159191040 | bytes 16777216 | tf_op jit(solution)/shard_map/attend_back/pallas_call | solution.py:235
  312.6 6.2 %all-to-all-start.2 = ((bf16[8,96,576]{2,1,0:T(8,128)(2,1)}), bf16[8,96,576]{2,1,0:T(8,128)(2,1)}, u32[]{:S(2)}, u32[]{:S(2)}) async-start(bf16[8,96,576]{2,1,0:T(8,128)(2,1)} %get-tuple-element.244), calls=%async_computation.3 | async-start | bytes 1966080 | tf_op jit(solution)/shard_map/all_to_all | solution.py:812
  320.4 13.3 %front_back.2 = (bf16[1,512,768]{2,1,0:T(8,128)(2,1)}, bf16[8,272,96]{2,1,0:T(8,128)(2,1)}) custom-call(s32[1]{0:T(128)} %bitcast.5.at_ref, s32[1]{0:T(128)} %get-tuple-element.357.len_ref, s32[1,1,528]{2,1,0:T(1,128)} %copy-done.48, bf16[8,272,96]{2,1,0:T(8,128)(2,1)} %bitcast.81, f32[1,256,768]{2,1,0:T(8,128)} %bitcast.83, ...), custom_call_target="tpu_custom_call" | custom-call | flops 3425697792 | bytes 4866048 | tf_op jit(solution)/shard_map/front_back/pallas_call | solution.py:606
  342.4 13.2 %front_back.3 = (bf16[1,512,768]{2,1,0:T(8,128)(2,1)}, bf16[8,272,96]{2,1,0:T(8,128)(2,1)}) custom-call(s32[1]{0:T(128)} %bitcast.5.at_ref, s32[1]{0:T(128)} %get-tuple-element.356.len_ref, s32[1,1,528]{2,1,0:T(1,128)} %copy-done.47, bf16[8,272,96]{2,1,0:T(8,128)(2,1)} %bitcast.82, f32[1,256,768]{2,1,0:T(8,128)} %bitcast.84, ...), custom_call_target="tpu_custom_call" | custom-call | flops 3425697792 | bytes 4866048 | tf_op jit(solution)/shard_map/front_back/pallas_call | solution.py:606
  372.6 4.4 %all-to-all-start.1 = ((bf16[8,272,96]{2,1,0:T(8,128)(2,1)}), bf16[8,272,96]{2,1,0:T(8,128)(2,1)}, u32[]{:S(2)}, u32[]{:S(2)}) async-start(bf16[8,272,96]{2,1,0:T(8,128)(2,1)} %add_convert_fusion.1), calls=%async_computation.2 | async-start | bytes 1114112 | tf_op jit(solution)/shard_map/all_to_all | solution.py:812
  (489 shorter events, 162.7 us)
Async XLA Ops:
  7.2 155.3 %all-gather.3.cloned.1.call-start = ((), (), s32[]{:S(2)}) async-start(), calls=%async_computation.5 | async-start | bytes 2654208 | tf_op jit(solution)/shard_map/all_gather | solution.py:908
  9.6 21.6 %collective-permute-start.1 = (bf16[1,1,1,272,96]{4,3,2,1,0:T(8,128)(2,1)S(1)}, bf16[1,1,1,272,96]{4,3,2,1,0:T(8,128)(2,1)S(1)}, u32[]{:S(2)}, u32[]{:S(2)}) collective-permute-start(bf16[1,1,1,272,96]{4,3,2,1,0:T(8,128)(2,1)S(1)} %bitcast.119), channel_id=1, source_target_pairs={{0,16},{4,20},{8,24},{12,28},{16,0},{20,4},{24,8},{28,12},{1,17},{... | collective-permute-start | bytes 156680 | tf_op jit(solution)/shard_map/ppermute | solution.py:749
  17.2 39.2 %collective-permute-start.8 = (bf16[2,256,768]{2,1,0:T(8,128)(2,1)}, bf16[2,256,768]{2,1,0:T(8,128)(2,1)}, u32[]{:S(2)}, u32[]{:S(2)}) collective-permute-start(bf16[2,256,768]{2,1,0:T(8,128)(2,1)} %refs_9_.1), channel_id=1, source_target_pairs={{0,2},{1,3},{2,0},{3,1},{4,6},{5,7},{6,4},{7,5},{8,10},{9,11},{10,... | collective-permute-start | bytes 2359304 | tf_op jit(solution)/shard_map/ppermute | solution.py:749
  44.3 276.1 %reduce-scatter.2.cloned.1.call-start = ((), (), s32[]{:S(2)}) async-start(), calls=%async_computation.4 | async-start | bytes 2654208 | tf_op jit(solution)/shard_map/reduce_scatter | solution.py:962
  64.7 32.9 %collective-permute-start.17 = (bf16[256,768]{1,0:T(8,128)(2,1)S(1)}, bf16[256,768]{1,0:T(8,128)(2,1)S(1)}, u32[]{:S(2)}, u32[]{:S(2)}) collective-permute-start(bf16[256,768]{1,0:T(8,128)(2,1)S(1)} %bitcast.85), channel_id=1, source_target_pairs={{0,2},{1,3},{2,0},{3,1},{4,6},{5,7},{6,4},{7,5},{8,10},{9,11},{10,... | collective-permute-start | bytes 1179656 | tf_op jit(solution)/shard_map/ppermute | solution.py:749
  75.8 21.7 %collective-permute-start.18 = (bf16[256,768]{1,0:T(8,128)(2,1)S(1)}, bf16[256,768]{1,0:T(8,128)(2,1)S(1)}, u32[]{:S(2)}, u32[]{:S(2)}) collective-permute-start(bf16[256,768]{1,0:T(8,128)(2,1)S(1)} %bitcast.86), channel_id=1, source_target_pairs={{0,1},{1,0},{2,3},{3,2},{4,5},{5,4},{6,7},{7,6},{8,9},{9,8},{10,11... | collective-permute-start | bytes 1179656 | tf_op jit(solution)/shard_map/ppermute | solution.py:749
  97.0 34.4 %collective-permute-start.16 = (bf16[768,192]{1,0:T(8,128)(2,1)}, bf16[768,192]{1,0:T(8,128)(2,1)S(1)}, u32[]{:S(2)}, u32[]{:S(2)}) collective-permute-start(bf16[768,192]{1,0:T(8,128)(2,1)} %collective-permute-done.14.refs_1_), channel_id=1, source_target_pairs={{0,1},{1,0},{2,3},{3,2},{4,5},{5,4},{6,7},{7,6},{8,9},{9,8},{10,11... | collective-permute-start | bytes 884744 | tf_op jit(solution)/shard_map/ppermute | solution.py:749
  97.2 35.0 %collective-permute-start.15 = (bf16[768,192]{1,0:T(8,128)(2,1)S(1)}, bf16[768,192]{1,0:T(8,128)(2,1)S(1)}, u32[]{:S(2)}, u32[]{:S(2)}) collective-permute-start(bf16[768,192]{1,0:T(8,128)(2,1)S(1)} %slice.154.refs_0_), channel_id=1, source_target_pairs={{0,1},{1,0},{2,3},{3,2},{4,5},{5,4},{6,7},{7,6},{8,9},{9,8},{10,11... | collective-permute-start | bytes 884744 | tf_op jit(solution)/shard_map/ppermute | solution.py:749
  197.7 27.7 %collective-permute-start.35 = (bf16[256,768]{1,0:T(8,128)(2,1)}, bf16[256,768]{1,0:T(8,128)(2,1)}, u32[]{:S(2)}, u32[]{:S(2)}) collective-permute-start(bf16[256,768]{1,0:T(8,128)(2,1)} %get-tuple-element.180), channel_id=1, source_target_pairs={{0,1},{1,0},{2,3},{3,2},{4,5},{5,4},{6,7},{7,6},{8,9},{9,8},{10,11... | collective-permute-start | bytes 1179656 | tf_op jit(solution)/shard_map/ppermute | solution.py:749
  199.6 25.8 %collective-permute-start.37 = (bf16[256,768]{1,0:T(8,128)(2,1)}, bf16[256,768]{1,0:T(8,128)(2,1)}, u32[]{:S(2)}, u32[]{:S(2)}) collective-permute-start(bf16[256,768]{1,0:T(8,128)(2,1)} %add_convert_fusion.3), channel_id=1, source_target_pairs={{0,2},{1,3},{2,0},{3,1},{4,6},{5,7},{6,4},{7,5},{8,10},{9,11},{10,... | collective-permute-start | bytes 1179656 | tf_op jit(solution)/shard_map/ppermute | solution.py:749
  231.3 34.1 %collective-permute-start.41 = (bf16[2,256,768]{2,1,0:T(8,128)(2,1)}, bf16[2,256,768]{2,1,0:T(8,128)(2,1)S(1)}, u32[]{:S(2)}, u32[]{:S(2)}) collective-permute-start(bf16[2,256,768]{2,1,0:T(8,128)(2,1)} %get-tuple-element.197), channel_id=1, source_target_pairs={{0,1},{1,0},{2,3},{3,2},{4,5},{5,4},{6,7},{7,6},{8,9},{9,8},{10,11... | collective-permute-start | bytes 2359304 | tf_op jit(solution)/shard_map/ppermute | solution.py:749
  231.8 34.8 %collective-permute-start.42 = (bf16[256,192]{1,0:T(8,128)(2,1)}, bf16[256,192]{1,0:T(8,128)(2,1)S(1)}, u32[]{:S(2)}, u32[]{:S(2)}) collective-permute-start(bf16[256,192]{1,0:T(8,128)(2,1)} %get-tuple-element.200), channel_id=1, source_target_pairs={{0,2},{1,3},{2,0},{3,1},{4,6},{5,7},{6,4},{7,5},{8,10},{9,11},{10,... | collective-permute-start | bytes 294920 | tf_op jit(solution)/shard_map/ppermute | solution.py:749
  232.4 36.0 %collective-permute-start.43 = (bf16[256,192]{1,0:T(8,128)(2,1)}, bf16[256,192]{1,0:T(8,128)(2,1)S(1)}, u32[]{:S(2)}, u32[]{:S(2)}) collective-permute-start(bf16[256,192]{1,0:T(8,128)(2,1)} %get-tuple-element.201), channel_id=1, source_target_pairs={{0,1},{1,0},{2,3},{3,2},{4,5},{5,4},{6,7},{7,6},{8,9},{9,8},{10,11... | collective-permute-start | bytes 294920 | tf_op jit(solution)/shard_map/ppermute | solution.py:749
  232.4 36.0 %collective-permute-start.44 = (bf16[256,192]{1,0:T(8,128)(2,1)}, bf16[256,192]{1,0:T(8,128)(2,1)S(1)}, u32[]{:S(2)}, u32[]{:S(2)}) collective-permute-start(bf16[256,192]{1,0:T(8,128)(2,1)} %get-tuple-element.202), channel_id=1, source_target_pairs={{0,3},{1,2},{2,1},{3,0},{4,7},{5,6},{6,5},{7,4},{8,11},{9,10},{10,... | collective-permute-start | bytes 294920 | tf_op jit(solution)/shard_map/ppermute | solution.py:749
  259.7 37.6 %collective-permute-start.47 = (bf16[256,768]{1,0:T(8,128)(2,1)}, bf16[256,768]{1,0:T(8,128)(2,1)}, u32[]{:S(2)}, u32[]{:S(2)}) collective-permute-start(bf16[256,768]{1,0:T(8,128)(2,1)} %get-tuple-element.212), channel_id=1, source_target_pairs={{0,2},{1,3},{2,0},{3,1},{4,6},{5,7},{6,4},{7,5},{8,10},{9,11},{10,... | collective-permute-start | bytes 1179656 | tf_op jit(solution)/shard_map/ppermute | solution.py:749
  260.3 52.3 %all-to-all-start = ((bf16[8,96,768]{2,1,0:T(8,128)(2,1)}), bf16[8,96,768]{2,1,0:T(8,128)(2,1)}, u32[]{:S(2)}, u32[]{:S(2)}) async-start(bf16[8,96,768]{2,1,0:T(8,128)(2,1)} %get-tuple-element.222), calls=%async_computation | async-start | bytes 2359296 | tf_op jit(solution)/shard_map/all_to_all | solution.py:812
  265.5 32.3 %collective-permute-start.48 = (bf16[256,768]{1,0:T(8,128)(2,1)}, bf16[256,768]{1,0:T(8,128)(2,1)}, u32[]{:S(2)}, u32[]{:S(2)}) collective-permute-start(bf16[256,768]{1,0:T(8,128)(2,1)} %get-tuple-element.213), channel_id=1, source_target_pairs={{0,1},{1,0},{2,3},{3,2},{4,5},{5,4},{6,7},{7,6},{8,9},{9,8},{10,11... | collective-permute-start | bytes 1179656 | tf_op jit(solution)/shard_map/ppermute | solution.py:749
  266.6 31.3 %collective-permute-start.49 = (bf16[256,768]{1,0:T(8,128)(2,1)}, bf16[256,768]{1,0:T(8,128)(2,1)}, u32[]{:S(2)}, u32[]{:S(2)}) collective-permute-start(bf16[256,768]{1,0:T(8,128)(2,1)} %get-tuple-element.214), channel_id=1, source_target_pairs={{0,3},{1,2},{2,1},{3,0},{4,7},{5,6},{6,5},{7,4},{8,11},{9,10},{10,... | collective-permute-start | bytes 1179656 | tf_op jit(solution)/shard_map/ppermute | solution.py:749
  268.3 35.8 %collective-permute-start.45 = (bf16[2,256,768]{2,1,0:T(8,128)(2,1)}, bf16[2,256,768]{2,1,0:T(8,128)(2,1)}, u32[]{:S(2)}, u32[]{:S(2)}) collective-permute-start(bf16[2,256,768]{2,1,0:T(8,128)(2,1)} %get-tuple-element.208), channel_id=1, source_target_pairs={{0,1},{1,0},{2,3},{3,2},{4,5},{5,4},{6,7},{7,6},{8,9},{9,8},{10,11... | collective-permute-start | bytes 2359304 | tf_op jit(solution)/shard_map/ppermute | solution.py:749
  268.3 44.3 %collective-permute-start.46 = (bf16[2,256,768]{2,1,0:T(8,128)(2,1)}, bf16[2,256,768]{2,1,0:T(8,128)(2,1)}, u32[]{:S(2)}, u32[]{:S(2)}) collective-permute-start(bf16[2,256,768]{2,1,0:T(8,128)(2,1)} %add_convert_fusion), channel_id=1, source_target_pairs={{0,2},{1,3},{2,0},{3,1},{4,6},{5,7},{6,4},{7,5},{8,10},{9,11},{10,... | collective-permute-start | bytes 2359304 | tf_op jit(solution)/shard_map/ppermute | solution.py:749
  305.4 28.3 %collective-permute-start.54 = (bf16[256,768]{1,0:T(8,128)(2,1)}, bf16[256,768]{1,0:T(8,128)(2,1)S(1)}, u32[]{:S(2)}, u32[]{:S(2)}) collective-permute-start(bf16[256,768]{1,0:T(8,128)(2,1)} %get-tuple-element.233), channel_id=1, source_target_pairs={{0,1},{1,0},{2,3},{3,2},{4,5},{5,4},{6,7},{7,6},{8,9},{9,8},{10,11... | collective-permute-start | bytes 1179656 | tf_op jit(solution)/shard_map/ppermute | solution.py:749
  310.4 23.3 %collective-permute-start.55 = (bf16[256,768]{1,0:T(8,128)(2,1)S(1)}, bf16[256,768]{1,0:T(8,128)(2,1)S(1)}, u32[]{:S(2)}, u32[]{:S(2)}) collective-permute-start(bf16[256,768]{1,0:T(8,128)(2,1)S(1)} %add_convert_fusion.2), channel_id=1, source_target_pairs={{0,2},{1,3},{2,0},{3,1},{4,6},{5,7},{6,4},{7,5},{8,10},{9,11},{10,... | collective-permute-start | bytes 1179656 | tf_op jit(solution)/shard_map/ppermute | solution.py:749
  312.6 53.4 %all-to-all-start.2 = ((bf16[8,96,576]{2,1,0:T(8,128)(2,1)}), bf16[8,96,576]{2,1,0:T(8,128)(2,1)}, u32[]{:S(2)}, u32[]{:S(2)}) async-start(bf16[8,96,576]{2,1,0:T(8,128)(2,1)} %get-tuple-element.244), calls=%async_computation.3 | async-start | bytes 1966080 | tf_op jit(solution)/shard_map/all_to_all | solution.py:812
  362.7 24.0 %collective-permute-start.70 = (bf16[96,1536]{1,0:T(8,128)(2,1)S(1)}, bf16[96,1536]{1,0:T(8,128)(2,1)S(1)}, u32[]{:S(2)}, u32[]{:S(2)}) collective-permute-start(bf16[96,1536]{1,0:T(8,128)(2,1)S(1)} %bitcast.115), channel_id=1, source_target_pairs={{0,1},{1,0},{2,3},{3,2},{4,5},{5,4},{6,7},{7,6},{8,9},{9,8},{10,11... | collective-permute-start | bytes 884744 | tf_op jit(solution)/shard_map/ppermute | solution.py:749
  (171 other events, 1615.6 us)
Sparse Core Ops, SparseCore 0:
  44.4 58.0 all-gather.2
  200.3 69.0 reduce-scatter.1
